TPU v7x, 32 devices: a whole 2x2x4 slice. The times are simulated.
32 devices in a mesh: group: 16 (over z, x, core), shard: 2 (over y).
Axes of the slice: x: 2, y: 2, z: 4, core: 2. Of those that a mesh axis runs over, the one named last changes fastest.
Arguments:
- owners: int32 [6], replicated, may hold values from 0 to 1, as said below
- mat_weight: bfloat16 [6, 128, 4096], P(None, 'shard'), may hold values from -0.09375 to 0.09375
- mat_grad: bfloat16 [16, 6, 128, 4096], P('group', None, 'shard'), may hold values from -2 to 2
- head_block_momentum: bfloat16 [6, 128, 4096], P(None, 'shard'), may hold values from -48 to 48
- emb_weight: bfloat16 [64, 4096], P('shard'), may hold values from -6 to 6
- emb_grad: bfloat16 [16, 64, 4096], P('group', 'shard'), may hold values from -2 to 2
- emb_first: float32 [64, 4096], P('shard'), may hold values from -6 to 6
- emb_second: float32 [64, 4096], P('shard'), may hold values from 0.1 to 10
- norm_weight: bfloat16 [2, 4096], P(None, 'shard'), may hold values from 0.5 to 1.5
- norm_grad: bfloat16 [16, 2, 4096], P('group', None, 'shard'), may hold values from -2 to 2
- norm_first: float32 [2, 4096], P(None, 'shard'), may hold values from -6 to 6
- norm_second: float32 [2, 4096], P(None, 'shard'), may hold values from 0.1 to 10
- qk_weight: bfloat16 [2, 128], replicated, may hold values from 0.5 to 1.5
- qk_grad: bfloat16 [16, 2, 128], P('group'), may hold values from -2 to 2
- qk_first: float32 [2, 128], replicated, may hold values from -6 to 6
- qk_second: float32 [2, 128], replicated, may hold values from 0.1 to 10
Outputs:
- new_weight: bfloat16 [6, 128, 4096], P(None, 'shard')
- new_moment: bfloat16 [6, 128, 4096], P(None, 'shard')
- owner_sums: float32 [2, 3], P('shard')
- emb_new: bfloat16 [64, 4096], P('shard')
- emb_first_new: float32 [64, 4096], P('shard')
- emb_second_new: float32 [64, 4096], P('shard')
- norm_new: bfloat16 [2, 4096], P(None, 'shard')
- norm_first_new: float32 [2, 4096], P(None, 'shard')
- norm_second_new: float32 [2, 4096], P(None, 'shard')
- qk_new: bfloat16 [2, 128], replicated
- qk_first_new: float32 [2, 128], replicated
- qk_second_new: float32 [2, 128], replicated
Inputs may be any that keep to these rules, and one draw needn't show every extreme that they name: `owners`: each shard rank owns at most 3 head blocks, and some rank owns exactly 3.
All inputs are finite; a program needn't handle non-finite values.
Results may differ from a plain program's by a relative error of at most 0.008.
Values may be sent and summed in bfloat16 or wider, within the bound.
A program may use at most 64 MiB of HBM per device.

v0:
```python
import math

import jax
import jax.numpy as jnp
from jax import lax
from jax.sharding import PartitionSpec as P

D = 4096
HEAD = 128
MATS = 6
NS_ITERS = 5


momentum_decay = 0.95
muon_rate = 0.02
weight_decay = 0.1
adam_rate = 0.01
beta_first = 0.9
beta_second = 0.95
adam_epsilon = 1e-08
bias_first = 1.0 - 0.9**10
bias_second = 1.0 - 0.95**10
norm_epsilon = 1e-07
quintic_a = 3.4445
quintic_b = -4.775
quintic_c = 2.0315


def orthogonalize(matrix):
    widened = matrix.astype(jnp.float32)
    iterate = (widened / (jnp.sqrt(jnp.sum(widened * widened)) + norm_epsilon)).astype(jnp.bfloat16)
    for sweep in range(NS_ITERS):
        gram = jnp.dot(iterate, iterate.T, preferred_element_type=jnp.float32).astype(jnp.bfloat16)
        squared = jnp.dot(gram, gram, preferred_element_type=jnp.float32)
        blend = (quintic_b * gram.astype(jnp.float32) + quintic_c * squared).astype(jnp.bfloat16)
        iterate = (
            quintic_a * iterate.astype(jnp.float32)
            + jnp.dot(blend, iterate, preferred_element_type=jnp.float32)
        ).astype(jnp.bfloat16)
    return iterate


def slot_energy(ortho, pushed):
    return jnp.sum(ortho.astype(jnp.float32) * pushed.astype(jnp.float32), axis=(1, 2)) / (
        HEAD * math.sqrt(D)
    )


def owner_slots(owners, capacity):
    order = jnp.arange(owners.shape[0], dtype=jnp.int32)
    same = (owners[:, None] == owners[None, :]) & (order[None, :] < order[:, None])
    position = jnp.sum(same.astype(jnp.int32), axis=1)
    return owners * capacity + position


def adamw(weight, grad_sum, first, second):
    first_new = beta_first * first + (1.0 - beta_first) * grad_sum
    second_new = beta_second * second + (1.0 - beta_second) * grad_sum * grad_sum
    wide_weight = weight.astype(jnp.float32)
    stepped = (
        first_new / bias_first / (jnp.sqrt(second_new / bias_second) + adam_epsilon)
        + weight_decay * wide_weight
    )
    return ((wide_weight - adam_rate * stepped).astype(jnp.bfloat16), first_new, second_new)


def on_device(
    owners,
    mat_weight,
    mat_grad,
    head_block_momentum,
    emb_weight,
    emb_grad,
    emb_first,
    emb_second,
    norm_weight,
    norm_grad,
    norm_first,
    norm_second,
    qk_weight,
    qk_grad,
    qk_first,
    qk_second,
):
    shards = lax.axis_size("shard")
    capacity = -(-MATS // shards)
    rows = mat_weight.shape[1]
    width = mat_weight.shape[2]
    muon_scale = 0.2 * math.sqrt(max(HEAD, D))
    local_grad = mat_grad[0].astype(jnp.float32)
    grad_total, emb_total, norm_total, qk_total = lax.psum(
        (
            local_grad,
            emb_grad[0].astype(jnp.float32),
            norm_grad[0].astype(jnp.float32),
            qk_grad[0].astype(jnp.float32),
        ),
        "group",
    )
    moment_wide = momentum_decay * head_block_momentum.astype(jnp.float32) + grad_total
    new_moment = moment_wide.astype(jnp.bfloat16)
    forwarded_rows = (grad_total + momentum_decay * moment_wide).astype(jnp.bfloat16)
    slots = owner_slots(owners, capacity)
    places = jnp.arange(shards * capacity, dtype=jnp.int32)
    gather_rows_back = (slots[:, None] == places[None, :]).astype(jnp.bfloat16)
    outgoing = jnp.einsum(
        "of,oyq->fyq", gather_rows_back, forwarded_rows, preferred_element_type=jnp.float32
    ).astype(jnp.bfloat16)
    outgoing = outgoing.reshape(shards, capacity, rows, width)
    items = lax.all_to_all(outgoing, "shard", split_axis=0, concat_axis=2, tiled=True)
    ortho = lax.map(orthogonalize, items[0])
    returned = lax.all_to_all(ortho[None], "shard", split_axis=2, concat_axis=0, tiled=True)
    returned, owner_sums = (returned, slot_energy(ortho, items[0])[None])
    kept_row_block = returned.reshape(shards * capacity, rows, width)
    muon_update = jnp.einsum(
        "ar,rpx->apx", gather_rows_back, kept_row_block, preferred_element_type=jnp.float32
    )
    new_weight = (
        mat_weight.astype(jnp.float32) * (1.0 - muon_rate * weight_decay)
        - muon_rate * muon_scale * muon_update
    ).astype(jnp.bfloat16)
    emb_new, emb_first_new, emb_second_new = adamw(emb_weight, emb_total, emb_first, emb_second)
    norm_new, norm_first_new, norm_second_new = adamw(
        norm_weight, norm_total, norm_first, norm_second
    )
    qk_new, qk_first_new, qk_second_new = adamw(qk_weight, qk_total, qk_first, qk_second)
    return (
        new_weight,
        new_moment,
        owner_sums,
        emb_new,
        emb_first_new,
        emb_second_new,
        norm_new,
        norm_first_new,
        norm_second_new,
        qk_new,
        qk_first_new,
        qk_second_new,
    )


def solution(mesh):
    placed = (
        P(),
        P(None, "shard", None),
        P("group", None, "shard", None),
        P(None, "shard", None),
        P("shard", None),
        P("group", "shard", None),
        P("shard", None),
        P("shard", None),
        P(None, "shard"),
        P("group", None, "shard"),
        P(None, "shard"),
        P(None, "shard"),
        P(),
        P("group", None, None),
        P(),
        P(),
    )
    return jax.shard_map(
        on_device,
        mesh=mesh,
        in_specs=placed,
        out_specs=(
            P(None, "shard", None),
            P(None, "shard", None),
            P("shard", None),
            P("shard", None),
            P("shard", None),
            P("shard", None),
            P(None, "shard"),
            P(None, "shard"),
            P(None, "shard"),
            P(),
            P(),
            P(),
        ),
        check_vma=False,
    )
```

profile of v0, /device:TPU:0, one launch (start us, length us, event | category | flops | bytes accessed | tf_op | source)
XLA Modules:
  0.0 362.9 jit_solution(13328973542228086273)
XLA Ops:
  7.2 5.3 %bitcast_convert_fusion = f32[6,64,4096]{2,1,0:T(8,128)} fusion(bf16[1,6,64,4096]{3,2,1,0:T(8,128)(2,1)} %param.20), kind=kLoop, calls=%fused_computation.76 | loop fusion | flops 1572864 | bytes 9437184 | tf_op jit(solution)/shard_map/convert_element_type | solution.py:90
  12.6 0.8 bitcast_convert_fusion.1
  14.2 149.8 %all-reduce.4.cloned.1.call-done = (f32[6,64,4096]{2,1,0:T(8,128)}, f32[32,4096]{1,0:T(8,128)}) async-done(((f32[6,64,4096]{2,1,0:T(8,128)}, f32[32,4096]{1,0:T(8,128)}), (f32[6,64,4096]{2,1,0:T(8,128)}, f32[32,4096]{1,0:T(8,128)})) %all-reduce.4.cloned.1.call-update) | async-done | bytes 6815760 | tf_op jit(solution)/shard_map/psum | solution.py:91
  164.0 5.8 %fusion.52 = (bf16[6,64,4096]{2,1,0:T(8,128)(2,1)}, bf16[6,64,4096]{2,1,0:T(8,128)(2,1)S(1)}) fusion(f32[6,64,4096]{2,1,0:T(8,128)} %get-tuple-element.98, bf16[6,64,4096]{2,1,0:T(8,128)(2,1)S(1)} %copy-done.1), kind=kLoop, calls=%fused_computation.71 | loop fusion | flops 11010048 | bytes 15728640 | tf_op jit(solution)/shard_map/convert_element_type | solution.py:101
  169.8 3.9 %convolution_convert_fusion.5 = bf16[6,64,4096]{2,0,1:T(8,128)(2,1)S(1)} fusion(bf16[6,64,4096]{2,1,0:T(8,128)(2,1)S(1)} %get-tuple-element.110, s32[6]{0:T(128)S(1)} %multiply_add_fusion.4), kind=kOutput, calls=%fused_computation.72 | convolution fusion | flops 20447268 | bytes 6291480 | tf_op jit(solution)/shard_map/of,oyq->fyq/dot_general | solution.py:106
  173.7 3.4 copy.61
  177.1 4.1 %all-to-all-start = ((bf16[2,3,64,4096]{3,2,1,0:T(8,128)(2,1)}), bf16[2,3,64,4096]{3,2,1,0:T(8,128)(2,1)S(1)}, u32[]{:S(2)}, u32[]{:S(2)}) async-start(bf16[2,3,64,4096]{3,2,1,0:T(8,128)(2,1)} %bitcast.5), calls=%async_computation | async-start | bytes 6291456 | tf_op jit(solution)/shard_map/all_to_all | solution.py:110
  181.3 60.2 %all-reduce = (f32[2,2048]{1,0:T(2,128)S(1)}, f32[2,128]{1,0:T(2,128)S(1)}) all-reduce(f32[2,2048]{1,0:T(2,128)S(1)} %bitcast_convert_fusion.2, f32[2,128]{1,0:T(2,128)S(1)} %bitcast_convert_fusion.3), channel_id=1, replica_groups=mesh['group'=16,'shard'=2] {'group'}, use_global_device_ids=true, to_apply=%region_7.8 | all-reduce | flops 4352 | bytes 34816 | tf_op jit(solution)/shard_map/psum | solution.py:91
  242.7 1.9 copy.62
  244.6 37.1 %while.10 = (s32[]{:T(128)}, bf16[3,128,4096]{2,1,0:T(8,128)(2,1)}, bf16[3,128,4096]{2,1,0:T(8,128)(2,1)}, s32[]{:T(128)}, f32[]{:T(128)}) while((s32[]{:T(128)}, bf16[3,128,4096]{2,1,0:T(8,128)(2,1)}, bf16[3,128,4096]{2,1,0:T(8,128)(2,1)}, s32[]{:T(128)}, f32[]{:T(128)}) %tuple.34), condition=%wide.region_4.0_spmd, body=%wide.region_2.4_spmd.sunk | while | flops 1380417536 | bytes 19336284 | solution.py:111
  244.6 2.4 fusion.152
  247.7 2.1 convolution_convert_fusion.11
  249.9 2.3 fusion.153
  255.6 1.5 fusion.157
  257.1 2.4 fusion.152
  260.2 2.0 convolution_convert_fusion.11
  262.2 2.2 fusion.153
  267.9 1.5 fusion.157
  269.4 2.4 fusion.152
  272.5 2.0 convolution_convert_fusion.11
  274.5 2.2 fusion.153
  280.2 1.5 fusion.157
  281.7 6.6 %copy.76 = bf16[3,128,4096]{2,0,1:T(4,128)(2,1)} copy(bf16[3,128,4096]{2,1,0:T(8,128)(2,1)} %get-tuple-element.29) | data formatting | bytes 6291456 | tf_op jit(solution)/shard_map/while | solution.py:111
  288.3 6.0 %all-to-all-start.1 = ((bf16[1,3,128,4096]{3,1,0,2:T(4,128)(2,1)}), bf16[1,3,128,4096]{3,1,0,2:T(4,128)(2,1)}, u32[]{:S(2)}, u32[]{:S(2)}) async-start(bf16[1,3,128,4096]{3,1,0,2:T(4,128)(2,1)} %bitcast.116), calls=%async_computation.1 | async-start | bytes 8388608 | tf_op jit(solution)/shard_map/all_to_all | solution.py:112
  294.3 1.3 fusion.57
  295.6 1.0 copy-done
  296.6 3.1 multiply_reduce_fusion
  300.2 37.3 %all-to-all-done.1 = bf16[1,3,128,4096]{3,1,0,2:T(4,128)(2,1)} async-done(((bf16[1,3,128,4096]{3,1,0,2:T(4,128)(2,1)}), bf16[1,3,128,4096]{3,1,0,2:T(4,128)(2,1)}, u32[]{:S(2)}, u32[]{:S(2)}) %all-to-all-start.1) | async-done | bytes 3145760 | tf_op jit(solution)/shard_map/all_to_all | solution.py:112
  337.5 4.5 %copy.64 = bf16[1,3,128,4096]{3,2,1,0:T(8,128)(2,1)S(1)} copy(bf16[1,3,128,4096]{3,1,0,2:T(4,128)(2,1)} %all-to-all-done.1) | data formatting | bytes 6291456 | tf_op jit(solution)/shard_map/all_to_all | solution.py:112
  342.2 1.7 copy-done.14
  343.9 8.8 %subtract_convert_fusion = bf16[6,64,4096]{2,0,1:T(8,128)(2,1)S(1)} fusion(bf16[6,64,4096]{2,1,0:T(8,128)(2,1)S(1)} %bitcast.119, bf16[6,64,4096]{2,1,0:T(8,128)(2,1)S(1)} %copy-done.14, s32[6]{0:T(128)S(1)} %multiply_add_fusion.4), kind=kOutput, calls=%fused_computation.67 | convolution fusion | flops 26738724 | bytes 9437208 | tf_op jit(solution)/shard_map/ar,rpx->apx/dot_general | solution.py:115
  352.6 3.4 copy.67
  (65 shorter events, 13.1 us)
Async XLA Ops:
  7.2 5.4 %copy-start.5 = (bf16[1,32,4096]{2,1,0:T(8,128)(2,1)S(1)}, bf16[1,32,4096]{2,1,0:T(8,128)(2,1)}, u32[]{:S(2)}) copy-start(bf16[1,32,4096]{2,1,0:T(8,128)(2,1)} %param.23) | copy-start | bytes 786436
  7.2 156.8 %all-reduce.4.cloned.1.call-start = ((), (), s32[]{:S(2)}) async-start(), calls=%async_computation.2 | async-start | bytes 13631488 | tf_op jit(solution)/shard_map/psum | solution.py:91
  13.4 0.7 copy-start.15
  13.4 150.6 %copy-start.1 = (bf16[6,64,4096]{2,1,0:T(8,128)(2,1)S(1)}, bf16[6,64,4096]{2,1,0:T(8,128)(2,1)}, u32[]{:S(2)}) copy-start(bf16[6,64,4096]{2,1,0:T(8,128)(2,1)} %param.21) | copy-start | bytes 9437188
  177.1 4.2 %copy-start.16 = (bf16[1,2,128]{2,1,0:T(2,128)(2,1)S(1)}, bf16[1,2,128]{2,1,0:T(2,128)(2,1)}, u32[]{:S(2)}) copy-start(bf16[1,2,128]{2,1,0:T(2,128)(2,1)} %param.31) | copy-start | bytes 1540
  177.1 4.2 %copy-start.9 = (bf16[1,2,2048]{2,1,0:T(2,128)(2,1)S(1)}, bf16[1,2,2048]{2,1,0:T(2,128)(2,1)}, u32[]{:S(2)}) copy-start(bf16[1,2,2048]{2,1,0:T(2,128)(2,1)} %param.27) | copy-start | bytes 24580
  177.1 64.4 %copy-start.11 = (f32[2,128]{1,0:T(2,128)S(1)}, f32[2,128]{1,0:T(2,128)}, u32[]{:S(2)}) copy-start(f32[2,128]{1,0:T(2,128)} %param.32) | copy-start | bytes 3076
  177.1 64.4 %copy-start.12 = (f32[2,128]{1,0:T(2,128)S(1)}, f32[2,128]{1,0:T(2,128)}, u32[]{:S(2)}) copy-start(f32[2,128]{1,0:T(2,128)} %param.33) | copy-start | bytes 3076
  177.1 64.4 %copy-start.13 = (bf16[2,128]{1,0:T(2,128)(2,1)S(1)}, bf16[2,128]{1,0:T(2,128)(2,1)}, u32[]{:S(2)}) copy-start(bf16[2,128]{1,0:T(2,128)(2,1)} %param.30) | copy-start | bytes 1540
  177.1 64.9 %copy-start.7 = (f32[2,2048]{1,0:T(2,128)S(1)}, f32[2,2048]{1,0:T(2,128)}, u32[]{:S(2)}) copy-start(f32[2,2048]{1,0:T(2,128)} %param.28) | copy-start | bytes 49156
  177.1 64.9 %copy-start.8 = (f32[2,2048]{1,0:T(2,128)S(1)}, f32[2,2048]{1,0:T(2,128)}, u32[]{:S(2)}) copy-start(f32[2,2048]{1,0:T(2,128)} %param.29) | copy-start | bytes 49156
  177.1 64.9 %copy-start.10 = (bf16[2,2048]{1,0:T(2,128)(2,1)S(1)}, bf16[2,2048]{1,0:T(2,128)(2,1)}, u32[]{:S(2)}) copy-start(bf16[2,2048]{1,0:T(2,128)(2,1)} %param.26) | copy-start | bytes 24580
  177.1 65.6 %all-to-all-start = ((bf16[2,3,64,4096]{3,2,1,0:T(8,128)(2,1)}), bf16[2,3,64,4096]{3,2,1,0:T(8,128)(2,1)S(1)}, u32[]{:S(2)}, u32[]{:S(2)}) async-start(bf16[2,3,64,4096]{3,2,1,0:T(8,128)(2,1)} %bitcast.5), calls=%async_computation | async-start | bytes 6291456 | tf_op jit(solution)/shard_map/all_to_all | solution.py:110
  288.3 6.0 %copy-start.2 = (f32[32,4096]{1,0:T(8,128)S(1)}, f32[32,4096]{1,0:T(8,128)}, u32[]{:S(2)}) copy-start(f32[32,4096]{1,0:T(8,128)} %param.24) | copy-start | bytes 1572868
  288.3 6.0 %copy-start.3 = (f32[32,4096]{1,0:T(8,128)S(1)}, f32[32,4096]{1,0:T(8,128)}, u32[]{:S(2)}) copy-start(f32[32,4096]{1,0:T(8,128)} %param.25) | copy-start | bytes 1572868
  288.3 6.0 %copy-start.4 = (f32[32,4096]{1,0:T(8,128)S(1)}, f32[32,4096]{1,0:T(8,128)}, u32[]{:S(2)}) copy-start(f32[32,4096]{1,0:T(8,128)} %get-tuple-element.99) | copy-start | bytes 1572868
  288.3 6.0 %copy-start.6 = (bf16[32,4096]{1,0:T(8,128)(2,1)S(1)}, bf16[32,4096]{1,0:T(8,128)(2,1)}, u32[]{:S(2)}) copy-start(bf16[32,4096]{1,0:T(8,128)(2,1)} %param.22) | copy-start | bytes 786436
  288.3 49.2 %all-to-all-start.1 = ((bf16[1,3,128,4096]{3,1,0,2:T(4,128)(2,1)}), bf16[1,3,128,4096]{3,1,0,2:T(4,128)(2,1)}, u32[]{:S(2)}, u32[]{:S(2)}) async-start(bf16[1,3,128,4096]{3,1,0,2:T(4,128)(2,1)} %bitcast.116), calls=%async_computation.1 | async-start | bytes 8388608 | tf_op jit(solution)/shard_map/all_to_all | solution.py:112
  294.3 2.4 copy-start
  342.0 1.9 copy-start.14
Sparse Core Ops, SparseCore 0:
  13.5 150.4 all-reduce.3
where the time goes:
time: 364 us; the launch traced here: 363 us
  waiting for transfers between devices  187 us (51%)
  blocking collectives  60.2 us (17%)
  matrix products  40.3 us (11%)
  other arithmetic  25.4 us (7%)
  local copies, waits for them, and re-layouts  23.3 us (6%)
  between operations  14.2 us (4%)
  starting transfers between devices  10.1 us (3%)
    psum x1, waiting for transfers between devices, on_device(): lax.psum((local_grad, emb_grad[0].astype(jnp.float32), norm_grad[0].astyp...  150 us
    psum x1, blocking collectives, on_device(): lax.psum((local_grad, emb_grad[0].astype(jnp.float32), norm_grad[0].astyp...  60.2 us
    all_to_all x1, waiting for transfers between devices, on_device(): lax.all_to_all(ortho[None], 'shard', split_axis=2, concat_axis=0, tiled=T...  37.3 us
    dot_general x15, matrix products, orthogonalize(): jnp.dot(blend, iterate, preferred_element_type=jnp.float32)  16.3 us
    dot_general x15, matrix products, orthogonalize(): jnp.dot(iterate, iterate.T, preferred_element_type=jnp.float32)  11.4 us
    dot_general x1, matrix products, on_device(): jnp.einsum('ar,rpx->apx', gather_rows_back, kept_row_block, preferred_ele...  8.75 us
  transfers between devices with their start and end apart: 3, of which 2 were waited for; matrix products, arithmetic and copies ran while one was open for 2% of the time, Pallas kernels for 0%

commit v1 on v0

--- a/solution.py
+++ b/solution.py
@@ -1,8 +1,11 @@
+import functools
 import math
 
 import jax
 import jax.numpy as jnp
 from jax import lax
+from jax.experimental import pallas as pl
+from jax.experimental.pallas import tpu as pltpu
 from jax.sharding import PartitionSpec as P
 
 D = 4096
@@ -140,7 +143,352 @@
     )
 
 
+SMALL_ROWS = 48
+HALF_MATS = -(-MATS // 2)
+TILE = 512
+
+
+def links_fit(groups, shards):
+    return groups & (groups - 1) == 0 and 4 <= groups <= 16 and shards == 2
+
+
+def wide(value):
+    return value.astype(jnp.float32)
+
+
+def linked_kernel(
+    bits,
+    grad_ref,
+    small_ref,
+    moment_hbm,
+    weight_hbm,
+    new_weight_hbm,
+    new_moment_hbm,
+    small_out,
+    energy_out,
+    moment,
+    weight,
+    total,
+    pushed,
+    gram0,
+    polynomial,
+    local_sem,
+    send_sem,
+    recv_sem,
+    *levels,
+):
+    landed, summed = levels[:bits], levels[bits:]
+    width = grad_ref.shape[2]
+    rows = grad_ref.shape[1]
+    chains = MATS + 1
+    widths = [width >> (level + 1) for level in range(bits)]
+    me = lax.axis_index("group")
+    shard = lax.axis_index("shard")
+    digit = [lax.rem(lax.div(me, 1 << b), 2) for b in range(bits)]
+    partner = [me + (1 << b) * (1 - 2 * digit[b]) for b in range(bits)]
+    other_shard = 1 - shard
+
+    plain = list(range(bits))
+    crossed = plain if bits < 3 else [0, 2, 1] + plain[3:]
+    orders = [crossed if c in (2, MATS) else plain for c in range(chains)]
+
+    def offset(c, level):
+        start = 0
+        for step in range(level + 1):
+            start = start + digit[orders[c][step]] * widths[step]
+        return pl.multiple_of(start, widths[-1])
+
+    barrier = pltpu.get_barrier_semaphore()
+    for b in range(bits):
+        pl.semaphore_signal(
+            barrier, inc=1, device_id=(partner[b], shard), device_id_type=pl.DeviceIdType.MESH
+        )
+    pl.semaphore_signal(
+        barrier, inc=1, device_id=(me, other_shard), device_id_type=pl.DeviceIdType.MESH
+    )
+    loads = [
+        pltpu.make_async_copy(moment_hbm, moment, local_sem.at[0]),
+        pltpu.make_async_copy(weight_hbm, weight, local_sem.at[1]),
+    ]
+    for load in loads:
+        load.start()
+    pl.semaphore_wait(barrier, bits + 1)
+
+    started = {}
+
+    def send(key, src, dst, device):
+        c, slot = key
+        copy = pltpu.make_async_remote_copy(
+            src_ref=src,
+            dst_ref=dst,
+            send_sem=send_sem.at[c, slot],
+            recv_sem=recv_sem.at[c, slot],
+            device_id=device,
+            device_id_type=pl.DeviceIdType.MESH,
+        )
+        copy.start()
+        started[key] = copy
+
+    def height(c):
+        return rows if c < MATS else SMALL_ROWS
+
+    def held(c, level):
+        if level >= 0:
+            return summed[level].at[c, pl.ds(0, height(c))]
+        return grad_ref.at[c] if c < MATS else small_ref
+
+    def scatter_start(c, level):
+        b = orders[c][level]
+        start = pl.multiple_of((1 - digit[b]) * widths[level], widths[level])
+        send(
+            (c, level),
+            held(c, level - 1).at[:, pl.ds(start, widths[level])],
+            landed[level].at[c, pl.ds(0, height(c))],
+            (partner[b], shard),
+        )
+
+    def scatter_finish(c, level):
+        started[(c, level)].wait_recv()
+        b = orders[c][level]
+        keep = digit[b] * widths[level]
+        tile = min(TILE, widths[level])
+        arrived = landed[level].at[c, pl.ds(0, height(c))]
+        mine = held(c, level - 1)
+        last = level == bits - 1
+        place = offset(c, level) if last else 0
+        target = total.at[c, pl.ds(0, height(c))] if last else held(c, level)
+
+        def add(i, carry):
+            at = pl.multiple_of(i * tile, tile)
+            value = wide(arrived[:, pl.ds(at, tile)]) + wide(
+                mine[:, pl.ds(pl.multiple_of(keep + at, tile), tile)]
+            )
+            target[:, pl.ds(pl.multiple_of(place + at, tile), tile)] = value.astype(jnp.bfloat16)
+            return carry
+
+        lax.fori_loop(0, widths[level] // tile, add, 0)
+
+    def gather_start(c, level):
+        region = total.at[c, pl.ds(0, height(c)), pl.ds(offset(c, level), widths[level])]
+        send((c, bits + level), region, region, (partner[orders[c][level]], shard))
+
+    def push(c, start):
+        def step(i, carry):
+            cols = pl.ds(pl.multiple_of(start + i * TILE, TILE), TILE)
+            grad = wide(total[c, :, cols])
+            moment_wide = momentum_decay * wide(moment[c, :, cols]) + grad
+            moment[c, :, cols] = moment_wide.astype(jnp.bfloat16)
+            pushed[c, 0:rows, cols] = (grad + momentum_decay * moment_wide).astype(jnp.bfloat16)
+            return carry
+
+        lax.fori_loop(0, widths[0] // TILE, step, 0)
+
+    stores = []
+    loaded = []
+
+    def stage(c, s):
+        if s == 0:
+            scatter_start(c, 0)
+        elif s < bits:
+            scatter_finish(c, s - 1)
+            scatter_start(c, s)
+        elif s == bits:
+            scatter_finish(c, bits - 1)
+            gather_start(c, bits - 1)
+        elif s < 2 * bits:
+            level = 2 * bits - s
+            started[(c, bits + level)].wait_recv()
+            gather_start(c, level - 1)
+            if level == 1 and c < MATS:
+                if not loaded:
+                    loads[0].wait()
+                    loaded.append(0)
+                push(c, offset(c, 0))
+                region = pl.ds(offset(c, 0), widths[0])
+                send(
+                    (c, 2 * bits),
+                    pushed.at[c, pl.ds(0, rows), region],
+                    pushed.at[c, pl.ds(rows, rows), region],
+                    (me, other_shard),
+                )
+        elif s == 2 * bits:
+            started[(c, bits)].wait_recv()
+            if c < MATS:
+                push(c, widths[0] - offset(c, 0))
+                store = pltpu.make_async_copy(
+                    moment.at[c], new_moment_hbm.at[c], local_sem.at[2 + c]
+                )
+                store.start()
+                stores.append(store)
+            else:
+                small_out[...] = total[c, 0:SMALL_ROWS]
+        elif s == 2 * bits + 1:
+            if c < MATS:
+                started[(c, 2 * bits)].wait_recv()
+                region = pushed.at[c, pl.ds(rows, rows), pl.ds(offset(c, 0), widths[0])]
+                send((c, 2 * bits + 1), region, region, (partner[orders[c][0]], shard))
+        elif s == 2 * bits + 2:
+            if c < MATS:
+                started[(c, 2 * bits + 1)].wait_recv()
+                block = pushed[c]
+                gram0[c] = lax.dot_general(
+                    block, block, (((1,), (1,)), ((), ())), preferred_element_type=jnp.float32
+                )
+
+    stages = 2 * bits + 3
+    for c in range(chains):
+        stage(c, 0)
+    for tick in range(1, stages + chains):
+        for c in range(chains):
+            s = tick - c
+            if 1 <= s < stages:
+                stage(c, s)
+
+    def narrow_dot(left, right):
+        return jnp.dot(
+            left.astype(jnp.bfloat16),
+            right.astype(jnp.bfloat16),
+            preferred_element_type=jnp.float32,
+        )
+
+    here = lax.broadcasted_iota(jnp.int32, (HEAD, HEAD), 0)
+    there = lax.broadcasted_iota(jnp.int32, (HEAD, HEAD), 1)
+    eye = jnp.where(here == there, 1.0, 0.0).astype(jnp.float32)
+    scales, grams, products = [], [], []
+    for c in range(MATS):
+        raw = gram0[c]
+        square = jnp.sum(jnp.sum(raw * eye, axis=1, keepdims=True), axis=0, keepdims=True)
+        scale = 1.0 / (jnp.sqrt(square) + norm_epsilon)
+        scales.append(scale)
+        grams.append(raw * scale * scale)
+        products.append(None)
+    for sweep in range(NS_ITERS):
+        squares = [narrow_dot(g, g) for g in grams]
+        blends = [
+            quintic_a * eye + quintic_b * g + quintic_c * s for g, s in zip(grams, squares)
+        ]
+        products = [
+            b if p is None else narrow_dot(b, p) for b, p in zip(blends, products)
+        ]
+        if sweep < NS_ITERS - 1:
+            halves = [narrow_dot(b, g) for b, g in zip(blends, grams)]
+            grams = [narrow_dot(h, b) for h, b in zip(halves, blends)]
+    for c in range(MATS):
+        scaled = products[c] * scales[c]
+        energy = jnp.sum(
+            jnp.sum(scaled * gram0[c], axis=1, keepdims=True), axis=0, keepdims=True
+        ) / (HEAD * math.sqrt(D))
+        energy_out[pl.ds(c, 1), :] = jnp.broadcast_to(energy, (1, 128))
+        polynomial[c] = scaled[0:rows].astype(jnp.bfloat16)
+
+    loads[1].wait()
+    muon_scale = 0.2 * math.sqrt(max(HEAD, D))
+    for c in range(MATS):
+
+        def update(i, carry):
+            cols = pl.ds(pl.multiple_of(i * TILE, TILE), TILE)
+            ortho = jnp.dot(
+                polynomial[c], pushed[c, :, cols], preferred_element_type=jnp.float32
+            ).astype(jnp.bfloat16)
+            weight[c, :, cols] = (
+                wide(weight[c, :, cols]) * (1.0 - muon_rate * weight_decay)
+                - muon_rate * muon_scale * wide(ortho)
+            ).astype(jnp.bfloat16)
+            return carry
+
+        lax.fori_loop(0, width // TILE, update, 0)
+        store = pltpu.make_async_copy(
+            weight.at[c], new_weight_hbm.at[c], local_sem.at[2 + MATS + c]
+        )
+        store.start()
+        stores.append(store)
+    for copy in started.values():
+        copy.wait_send()
+    for store in stores:
+        store.wait()
+
+
+def linked_device(
+    groups,
+    owners,
+    mat_weight,
+    mat_grad,
+    head_block_momentum,
+    emb_weight,
+    emb_grad,
+    emb_first,
+    emb_second,
+    norm_weight,
+    norm_grad,
+    norm_first,
+    norm_second,
+    qk_weight,
+    qk_grad,
+    qk_first,
+    qk_second,
+):
+    bits = groups.bit_length() - 1
+    blocks, rows, width = mat_weight.shape
+    emb_rows = emb_weight.shape[0]
+    gains = norm_weight.shape[1]
+    heads = qk_weight.shape[1]
+    extra = jnp.concatenate([norm_grad[0], qk_grad[0]], axis=1)
+    extra = jnp.pad(extra, ((0, SMALL_ROWS - emb_rows - 2), (0, width - gains - heads)))
+    small = jnp.concatenate([emb_grad[0], extra], axis=0)
+    levels = [width >> (level + 1) for level in range(bits)]
+    in_vmem = pl.BlockSpec(memory_space=pltpu.VMEM)
+    anywhere = pl.BlockSpec(memory_space=pl.ANY)
+    block_shape = (blocks, rows, width)
+    new_weight, new_moment, small_sum, energy = pl.pallas_call(
+        functools.partial(linked_kernel, bits),
+        out_shape=(
+            jax.ShapeDtypeStruct(block_shape, jnp.bfloat16),
+            jax.ShapeDtypeStruct(block_shape, jnp.bfloat16),
+            jax.ShapeDtypeStruct((SMALL_ROWS, width), jnp.bfloat16),
+            jax.ShapeDtypeStruct((8, 128), jnp.float32),
+        ),
+        in_specs=[in_vmem, in_vmem, anywhere, anywhere],
+        out_specs=(anywhere, anywhere, in_vmem, in_vmem),
+        scratch_shapes=[
+            pltpu.VMEM(block_shape, jnp.bfloat16),
+            pltpu.VMEM(block_shape, jnp.bfloat16),
+            pltpu.VMEM((blocks + 1, rows, width), jnp.bfloat16),
+            pltpu.VMEM((blocks, 2 * rows, width), jnp.bfloat16),
+            pltpu.VMEM((blocks, HEAD, HEAD), jnp.float32),
+            pltpu.VMEM((blocks, rows, HEAD), jnp.bfloat16),
+            pltpu.SemaphoreType.DMA((2 + 2 * blocks,)),
+            pltpu.SemaphoreType.DMA((blocks + 1, 2 * bits + 2)),
+            pltpu.SemaphoreType.DMA((blocks + 1, 2 * bits + 2)),
+        ]
+        + [pltpu.VMEM((blocks + 1, rows, part), jnp.bfloat16) for part in levels]
+        + [pltpu.VMEM((blocks + 1, rows, part), jnp.bfloat16) for part in levels[:-1]],
+        compiler_params=pltpu.CompilerParams(
+            collective_id=0, has_side_effects=True, vmem_limit_bytes=56 * 1024 * 1024
+        ),
+    )(mat_grad[0], small, head_block_momentum, mat_weight)
+    small_sum = small_sum.astype(jnp.float32)
+    emb_total = small_sum[:emb_rows]
+    norm_total = small_sum[emb_rows : emb_rows + 2, :gains]
+    qk_total = small_sum[emb_rows : emb_rows + 2, gains : gains + heads]
+    slots = owner_slots(owners, HALF_MATS)
+    mine = lax.axis_index("shard") * HALF_MATS + jnp.arange(HALF_MATS, dtype=jnp.int32)
+    owner_sums = jnp.sum(
+        jnp.where(slots[None, :] == mine[:, None], energy[:blocks, 0][None, :], 0.0), axis=1
+    )[None]
+    return (
+        new_weight,
+        new_moment,
+        owner_sums,
+        *adamw(emb_weight, emb_total, emb_first, emb_second),
+        *adamw(norm_weight, norm_total, norm_first, norm_second),
+        *adamw(qk_weight, qk_total, qk_first, qk_second),
+    )
+
+
 def solution(mesh):
+    plan = on_device
+    if links_fit(mesh.shape["group"], mesh.shape["shard"]):
+        plan = functools.partial(linked_device, mesh.shape["group"])
     placed = (
         P(),
         P(None, "shard", None),
@@ -160,7 +508,7 @@
         P(),
     )
     return jax.shard_map(
-        on_device,
+        plan,
         mesh=mesh,
         in_specs=placed,
         out_specs=(

time: 364 us -> 102 us (0.28)
  waiting for transfers between devices: 187 us -> 0 us
  Pallas kernels: 0 us -> 85.8 us
  blocking collectives: 60.2 us -> 0 us
  matrix products: 40.3 us -> 0 us
  local copies, waits for them, and re-layouts: 23.3 us -> 5.69 us
  other arithmetic: 25.4 us -> 8.15 us
  between operations: 14.2 us -> 0.75 us
  starting transfers between devices: 10.1 us -> 0 us
    psum x1 -> x0, waiting for transfers between devices: 150 us -> none  [on_device(): lax.psum((local_grad, emb_grad[0].astype(jnp.float32), norm_grad[0].astyp...]
    pallas_call x0 -> x1, Pallas kernels: none -> 85.8 us  [linked_device(): pl.pallas_call(functools.partial(linked_kernel, bits), out_shape=(jax.Sha...]
    psum x1 -> x0, blocking collectives: 60.2 us -> none  [on_device(): lax.psum((local_grad, emb_grad[0].astype(jnp.float32), norm_grad[0].astyp...]
    dot_general x32 -> x0, matrix products: 40.3 us -> none  [the longest x15 16.3 us: orthogonalize(): jnp.dot(blend, iterate, preferred_element_type=jnp.float32)]
    all_to_all x2 -> x0, waiting for transfers between devices: 37.3 us -> none  [the longest x1 37.3 us: on_device(): lax.all_to_all(ortho[None], 'shard', split_axis=2, concat_axis=0, tiled=T...]
    convert_element_type x5 -> x1, other arithmetic: 12 us -> 1.05 us  [linked_device(): small_sum = small_sum.astype(jnp.float32)]
    all_to_all x2 -> x0, starting transfers between devices: 10.1 us -> none  [the longest x1 5.97 us: on_device(): lax.all_to_all(ortho[None], 'shard', split_axis=2, concat_axis=0, tiled=T...]
    reduce_sum x4 -> x1, other arithmetic: 10.2 us -> 0.69 us  [linked_device(): jnp.sum(jnp.where(slots[None, :] == mine[:, None], energy[:blocks, 0][Non...]
  transfers between devices with their start and end apart: 3 -> 0, of which waited for: 2 -> 0; matrix products, arithmetic and copies ran while one was open for 2% -> 0% of each run, Pallas kernels for 0% -> 0%
where the time goes in v1:
time: 102 us; the launch traced here: 100 us
  Pallas kernels  85.8 us (84%)
  other arithmetic  8.15 us (8%)
  local copies, waits for them, and re-layouts  5.69 us (6%)
    pallas_call x1, Pallas kernels, linked_device(): pl.pallas_call(functools.partial(linked_kernel, bits), out_shape=(jax.Sha...  85.8 us
    unnamed x22, local copies, waits for them, and re-layouts  4.74 us
    convert_element_type x3, other arithmetic, adamw(): (wide_weight - adam_rate * stepped).astype(jnp.bfloat16)  3.76 us

profile of v1, /device:TPU:0, one launch (start us, length us, event | category | flops | bytes accessed | tf_op | source)
XLA Modules:
  0.0 100.3 jit_solution(4478650596472610797)
XLA Ops:
  0.6 0.7 fusion.9
  1.4 1.7 %pad_maximum_fusion.small_ref = bf16[48,4096]{1,0:T(8,128)(2,1)} fusion(bf16[16,4096]{1,0:T(8,128)(2,1)S(1)} %fusion.9, bf16[32,4096]{1,0:T(8,128)(2,1)} %bitcast.6), kind=kLoop, calls=%fused_computation.8 | loop fusion | flops 786432 | bytes 786432 | tf_op jit(solution)/shard_map/concatenate | solution.py:437
  3.1 0.0 copy-start.9
  3.1 0.0 copy-start.2
  3.1 85.8 %shard_map.247 = (bf16[6,64,4096]{2,1,0:T(8,128)(2,1)}, bf16[6,64,4096]{2,1,0:T(8,128)(2,1)}, bf16[48,4096]{1,0:T(8,128)(2,1)}, f32[8,128]{1,0:T(8,128)}) custom-call(bf16[6,64,4096]{2,1,0:T(8,128)(2,1)} %bitcast.5, bf16[48,4096]{1,0:T(8,128)(2,1)} %pad_maximum_fusion.small_ref, bf16[6,64,4096]{2,1,0:T(8,128)(2,1)} %moment_hbm.1, bf16[6,64,4096]{2,1,0:T(8,128)(2,1)} %weight_hbm.1), custom_call_target="tpu_custom_call" | custom-call | tf_op jit(solution)/shard_map/pallas_call | solution.py:442
  88.9 0.0 copy-start.3
  88.9 0.0 copy-start.4
  88.9 0.0 copy-start.5
  88.9 0.0 copy-start.6
  88.9 0.0 copy-start.7
  88.9 0.0 copy-start.8
  88.9 0.0 copy-start.1
  89.0 1.0 slice_reduce_fusion
  89.9 0.0 copy-done.9
  89.9 0.2 convert_reduce_fusion
  90.1 0.7 select_reduce_fusion
  90.8 1.0 %convert_element_type.28 = f32[48,4096]{1,0:T(8,128)S(1)} convert(bf16[48,4096]{1,0:T(8,128)(2,1)} %get-tuple-element.19) | non-fusion elementwise | flops 196608 | bytes 1179648 | tf_op jit(solution)/shard_map/convert_element_type | solution.py:469
  91.9 0.0 copy-done.2
  91.9 2.5 %fusion.2 = (bf16[32,4096]{1,0:T(8,128)(2,1)}, f32[32,4096]{1,0:T(8,128)}, f32[32,4096]{1,0:T(8,128)}) fusion(bf16[32,4096]{1,0:T(8,128)(2,1)S(1)} %copy-done.2, f32[48,4096]{1,0:T(8,128)S(1)} %convert_element_type.28, f32[32,4096]{1,0:T(8,128)} %param.22, f32[32,4096]{1,0:T(8,128)} %param.23), kind=kLoop, calls=%fused_computation.5 | loop fusion | flops 2228224 | bytes 3145728 | tf_op jit(solution)/shard_map/convert_element_type | solution.py:67
  94.4 0.0 copy-done.3
  94.4 0.0 copy-done.4
  94.4 0.0 copy-done.5
  94.4 0.7 fusion.13
  95.1 0.0 copy-done.6
  95.1 0.0 copy-done.7
  95.1 0.0 copy-done.8
  95.1 0.6 fusion.18
  95.7 0.0 copy-done.1
  95.7 0.0 copy-start
  95.7 1.7 %copy.30 = bf16[6,64,4096]{2,1,0:T(8,128)(2,1)} copy(bf16[6,64,4096]{2,1,0:T(8,128)(2,1)S(1)} %copy-done.1) | data formatting | bytes 6291456
  97.3 1.4 %copy-done = bf16[6,64,4096]{2,1,0:T(8,128)(2,1)S(1)} copy-done((bf16[6,64,4096]{2,1,0:T(8,128)(2,1)S(1)}, bf16[6,64,4096]{2,1,0:T(8,128)(2,1)}, u32[]{:S(2)}) %copy-start) | copy-done | bytes 3145752
  98.7 1.7 %copy.31 = bf16[6,64,4096]{2,1,0:T(8,128)(2,1)} copy(bf16[6,64,4096]{2,1,0:T(8,128)(2,1)S(1)} %copy-done) | data formatting | bytes 6291456
  (2 shorter events, 0.0 us)
Async XLA Ops:
  3.1 86.8 %copy-start.9 = (s32[6]{0:T(128)S(1)}, s32[6]{0:T(128)}, u32[]{:S(2)}) copy-start(s32[6]{0:T(128)} %param.16) | copy-start | bytes 76
  3.1 88.8 %copy-start.2 = (bf16[32,4096]{1,0:T(8,128)(2,1)S(1)}, bf16[32,4096]{1,0:T(8,128)(2,1)}, u32[]{:S(2)}) copy-start(bf16[32,4096]{1,0:T(8,128)(2,1)} %param.20) | copy-start | bytes 786436
  88.9 5.5 %copy-start.3 = (f32[2,2048]{1,0:T(2,128)S(1)}, f32[2,2048]{1,0:T(2,128)}, u32[]{:S(2)}) copy-start(f32[2,2048]{1,0:T(2,128)} %param.26) | copy-start | bytes 49156
  88.9 5.5 %copy-start.4 = (f32[2,2048]{1,0:T(2,128)S(1)}, f32[2,2048]{1,0:T(2,128)}, u32[]{:S(2)}) copy-start(f32[2,2048]{1,0:T(2,128)} %param.27) | copy-start | bytes 49156
  88.9 5.5 %copy-start.5 = (bf16[2,2048]{1,0:T(2,128)(2,1)S(1)}, bf16[2,2048]{1,0:T(2,128)(2,1)}, u32[]{:S(2)}) copy-start(bf16[2,2048]{1,0:T(2,128)(2,1)} %param.24) | copy-start | bytes 24580
  88.9 6.2 %copy-start.6 = (f32[2,128]{1,0:T(2,128)S(1)}, f32[2,128]{1,0:T(2,128)}, u32[]{:S(2)}) copy-start(f32[2,128]{1,0:T(2,128)} %param.30) | copy-start | bytes 3076
  88.9 6.2 %copy-start.7 = (f32[2,128]{1,0:T(2,128)S(1)}, f32[2,128]{1,0:T(2,128)}, u32[]{:S(2)}) copy-start(f32[2,128]{1,0:T(2,128)} %param.31) | copy-start | bytes 3076
  88.9 6.1 %copy-start.8 = (bf16[2,128]{1,0:T(2,128)(2,1)S(1)}, bf16[2,128]{1,0:T(2,128)(2,1)}, u32[]{:S(2)}) copy-start(bf16[2,128]{1,0:T(2,128)(2,1)} %param.28) | copy-start | bytes 1540
  88.9 6.7 %copy-start.1 = (bf16[6,64,4096]{2,1,0:T(8,128)(2,1)S(1)}, bf16[6,64,4096]{2,1,0:T(8,128)(2,1)}, u32[]{:S(2)}) copy-start(bf16[6,64,4096]{2,1,0:T(8,128)(2,1)} %get-tuple-element.41) | copy-start | bytes 9437188
  95.7 3.0 %copy-start = (bf16[6,64,4096]{2,1,0:T(8,128)(2,1)S(1)}, bf16[6,64,4096]{2,1,0:T(8,128)(2,1)}, u32[]{:S(2)}) copy-start(bf16[6,64,4096]{2,1,0:T(8,128)(2,1)} %get-tuple-element.42) | copy-start | bytes 9437188

commit v2 on v1

v2 whole, which is shorter than its diff:
```python
import functools
import math

import jax
import jax.numpy as jnp
from jax import lax
from jax.experimental import pallas as pl
from jax.experimental.pallas import tpu as pltpu
from jax.sharding import PartitionSpec as P

D = 4096
HEAD = 128
MATS = 6
NS_ITERS = 5


momentum_decay = 0.95
muon_rate = 0.02
weight_decay = 0.1
adam_rate = 0.01
beta_first = 0.9
beta_second = 0.95
adam_epsilon = 1e-08
bias_first = 1.0 - 0.9**10
bias_second = 1.0 - 0.95**10
norm_epsilon = 1e-07
quintic_a = 3.4445
quintic_b = -4.775
quintic_c = 2.0315


def orthogonalize(matrix):
    widened = matrix.astype(jnp.float32)
    iterate = (widened / (jnp.sqrt(jnp.sum(widened * widened)) + norm_epsilon)).astype(jnp.bfloat16)
    for sweep in range(NS_ITERS):
        gram = jnp.dot(iterate, iterate.T, preferred_element_type=jnp.float32).astype(jnp.bfloat16)
        squared = jnp.dot(gram, gram, preferred_element_type=jnp.float32)
        blend = (quintic_b * gram.astype(jnp.float32) + quintic_c * squared).astype(jnp.bfloat16)
        iterate = (
            quintic_a * iterate.astype(jnp.float32)
            + jnp.dot(blend, iterate, preferred_element_type=jnp.float32)
        ).astype(jnp.bfloat16)
    return iterate


def slot_energy(ortho, pushed):
    return jnp.sum(ortho.astype(jnp.float32) * pushed.astype(jnp.float32), axis=(1, 2)) / (
        HEAD * math.sqrt(D)
    )


def owner_slots(owners, capacity):
    order = jnp.arange(owners.shape[0], dtype=jnp.int32)
    same = (owners[:, None] == owners[None, :]) & (order[None, :] < order[:, None])
    position = jnp.sum(same.astype(jnp.int32), axis=1)
    return owners * capacity + position


def adamw(weight, grad_sum, first, second):
    first_new = beta_first * first + (1.0 - beta_first) * grad_sum
    second_new = beta_second * second + (1.0 - beta_second) * grad_sum * grad_sum
    wide_weight = weight.astype(jnp.float32)
    stepped = (
        first_new / bias_first / (jnp.sqrt(second_new / bias_second) + adam_epsilon)
        + weight_decay * wide_weight
    )
    return ((wide_weight - adam_rate * stepped).astype(jnp.bfloat16), first_new, second_new)


def on_device(
    owners,
    mat_weight,
    mat_grad,
    head_block_momentum,
    emb_weight,
    emb_grad,
    emb_first,
    emb_second,
    norm_weight,
    norm_grad,
    norm_first,
    norm_second,
    qk_weight,
    qk_grad,
    qk_first,
    qk_second,
):
    shards = lax.axis_size("shard")
    capacity = -(-MATS // shards)
    rows = mat_weight.shape[1]
    width = mat_weight.shape[2]
    muon_scale = 0.2 * math.sqrt(max(HEAD, D))
    local_grad = mat_grad[0].astype(jnp.float32)
    grad_total, emb_total, norm_total, qk_total = lax.psum(
        (
            local_grad,
            emb_grad[0].astype(jnp.float32),
            norm_grad[0].astype(jnp.float32),
            qk_grad[0].astype(jnp.float32),
        ),
        "group",
    )
    moment_wide = momentum_decay * head_block_momentum.astype(jnp.float32) + grad_total
    new_moment = moment_wide.astype(jnp.bfloat16)
    forwarded_rows = (grad_total + momentum_decay * moment_wide).astype(jnp.bfloat16)
    slots = owner_slots(owners, capacity)
    places = jnp.arange(shards * capacity, dtype=jnp.int32)
    gather_rows_back = (slots[:, None] == places[None, :]).astype(jnp.bfloat16)
    outgoing = jnp.einsum(
        "of,oyq->fyq", gather_rows_back, forwarded_rows, preferred_element_type=jnp.float32
    ).astype(jnp.bfloat16)
    outgoing = outgoing.reshape(shards, capacity, rows, width)
    items = lax.all_to_all(outgoing, "shard", split_axis=0, concat_axis=2, tiled=True)
    ortho = lax.map(orthogonalize, items[0])
    returned = lax.all_to_all(ortho[None], "shard", split_axis=2, concat_axis=0, tiled=True)
    returned, owner_sums = (returned, slot_energy(ortho, items[0])[None])
    kept_row_block = returned.reshape(shards * capacity, rows, width)
    muon_update = jnp.einsum(
        "ar,rpx->apx", gather_rows_back, kept_row_block, preferred_element_type=jnp.float32
    )
    new_weight = (
        mat_weight.astype(jnp.float32) * (1.0 - muon_rate * weight_decay)
        - muon_rate * muon_scale * muon_update
    ).astype(jnp.bfloat16)
    emb_new, emb_first_new, emb_second_new = adamw(emb_weight, emb_total, emb_first, emb_second)
    norm_new, norm_first_new, norm_second_new = adamw(
        norm_weight, norm_total, norm_first, norm_second
    )
    qk_new, qk_first_new, qk_second_new = adamw(qk_weight, qk_total, qk_first, qk_second)
    return (
        new_weight,
        new_moment,
        owner_sums,
        emb_new,
        emb_first_new,
        emb_second_new,
        norm_new,
        norm_first_new,
        norm_second_new,
        qk_new,
        qk_first_new,
        qk_second_new,
    )


SMALL_ROWS = 48
HALF_MATS = -(-MATS // 2)
TILE = 512
PIECES = 2
ORDER = (
    0, 1, 2, 3, 4, 5, 6, 7, 8, 9, 10, 11, 12, 13, 0, 1, 2, 3, 4, 5, 6, 7, 0, 8, 9, 1, 10, 11,
    2, 0, 12, 13, 1, 3, 2, 4, 0, 1, 5, 3, 2, 6, 4, 0, 7, 1, 5, 3, 8, 2, 6, 9, 4, 0, 10, 7, 1,
    11, 5, 3, 12, 8, 13, 2, 6, 0, 9, 4, 1, 10, 0, 7, 2, 5, 11, 1, 3, 12, 14, 2, 8, 13, 6, 9,
    14, 3, 15, 4, 10, 7, 5, 3, 15, 16, 8, 11, 4, 12, 13, 6, 5, 16, 17, 4, 7, 9, 10, 5, 6, 8,
    11, 17, 18, 12, 13, 9, 7, 6, 10, 11, 18, 8, 19, 7, 9, 12, 13, 8, 10, 19, 20, 11, 9, 10,
    12, 28, 13, 20, 21, 11, 12, 28, 22, 13, 21, 28, 28, 22, 23, 28, 28, 28, 23, 24, 28, 25,
    24, 25, 29, 29, 29, 29, 29, 29, 29, 29,
)


def links_fit(groups, shards):
    return groups == 16 and shards == 2


def wide(value):
    return value.astype(jnp.float32)


def linked_kernel(
    bits,
    norm_ref,
    qk_ref,
    grad_hbm,
    emb_hbm,
    moment_hbm,
    weight_hbm,
    new_weight_hbm,
    new_moment_hbm,
    small_out,
    energy_out,
    grad,
    moment,
    weight,
    small,
    total,
    pushed,
    gram0,
    gram,
    product,
    polynomial,
    local_sem,
    send_sem,
    recv_sem,
    *levels,
):
    landed, summed = levels[:bits], levels[bits:]
    rows, width = grad.shape[1], grad.shape[2] // PIECES
    chains = (MATS + 1) * PIECES
    widths = [width >> (level + 1) for level in range(bits)]
    me = lax.axis_index("group")
    shard = lax.axis_index("shard")
    digit = [lax.rem(lax.div(me, 1 << b), 2) for b in range(bits)]
    partner = [me + (1 << b) * (1 - 2 * digit[b]) for b in range(bits)]
    other_shard = 1 - shard
    offsets = []
    for level in range(bits):
        before = offsets[-1] if offsets else 0
        offsets.append(before + digit[level] * widths[level])

    barrier = pltpu.get_barrier_semaphore()
    for b in range(bits):
        pl.semaphore_signal(
            barrier, inc=1, device_id=(partner[b], shard), device_id_type=pl.DeviceIdType.MESH
        )
    pl.semaphore_signal(
        barrier, inc=1, device_id=(me, other_shard), device_id_type=pl.DeviceIdType.MESH
    )
    loads = {("grad", b): pltpu.make_async_copy(
        grad_hbm.at[b], grad.at[b], local_sem.at[3 + b]) for b in range(MATS)}
    loads["small"] = pltpu.make_async_copy(
        emb_hbm, small.at[pl.ds(0, emb_hbm.shape[0])], local_sem.at[0])
    loads["moment"] = pltpu.make_async_copy(moment_hbm, moment, local_sem.at[1])
    loads["weight"] = pltpu.make_async_copy(weight_hbm, weight, local_sem.at[2])
    for load in loads.values():
        load.start()
    extra = SMALL_ROWS - emb_hbm.shape[0]
    small[pl.ds(emb_hbm.shape[0], extra), :] = jnp.zeros((extra, small.shape[1]), jnp.bfloat16)
    place = 0
    for part in (norm_ref, qk_ref):
        tall = jnp.concatenate(
            [wide(part[...]), jnp.zeros((extra - 2, part.shape[1]), jnp.float32)], axis=0
        )
        small[pl.ds(emb_hbm.shape[0], extra), pl.ds(place, part.shape[1])] = tall.astype(
            jnp.bfloat16
        )
        place += part.shape[1]
    pl.semaphore_wait(barrier, bits + 1)

    def ready(key):
        if key in loads:
            loads.pop(key).wait()

    started = {}

    def send(c, slot, src, dst, device):
        copy = pltpu.make_async_remote_copy(
            src_ref=src,
            dst_ref=dst,
            send_sem=send_sem.at[c, slot],
            recv_sem=recv_sem.at[c, slot],
            device_id=device,
            device_id_type=pl.DeviceIdType.MESH,
        )
        copy.start()
        started[(c, slot)] = copy

    def block_of(c):
        return c // PIECES, (c % PIECES) * width

    def height(c):
        return rows if c < MATS * PIECES else SMALL_ROWS

    def held(c, level, own):
        block, base = block_of(c)
        if level >= 0:
            return summed[level].at[c, pl.ds(0, height(c))], 0
        if block == MATS:
            return small, base
        return (grad if own else grad_hbm).at[block], base

    def at_multiple(value, step):
        return value if isinstance(value, int) else pl.multiple_of(value, step)

    def scatter_start(c, level):
        if block_of(c)[0] == MATS:
            ready("small")
        source, base = held(c, level - 1, False)
        start = at_multiple(base + (1 - digit[level]) * widths[level], widths[level])
        send(
            c,
            level,
            source.at[:, pl.ds(start, widths[level])],
            landed[level].at[c, pl.ds(0, height(c))],
            (partner[level], shard),
        )

    def scatter_finish(c, level):
        block, base = block_of(c)
        if level == 0:
            ready(("grad", block))
        started[(c, level)].wait_recv()
        mine, keep = held(c, level - 1, True)
        keep = keep + digit[level] * widths[level]
        tile = min(TILE, widths[level])
        arrived = landed[level].at[c, pl.ds(0, height(c))]
        if level == bits - 1:
            target, place = total.at[block, pl.ds(0, height(c))], base + offsets[level]
        else:
            target, place = summed[level].at[c, pl.ds(0, height(c))], 0

        def add(i, carry):
            at = at_multiple(i * tile, tile)
            value = wide(arrived[:, pl.ds(at, tile)]) + wide(
                mine[:, pl.ds(at_multiple(keep + at, tile), tile)]
            )
            target[:, pl.ds(at_multiple(place + at, tile), tile)] = value.astype(jnp.bfloat16)
            return carry

        if widths[level] == tile:
            add(0, 0)
        else:
            lax.fori_loop(0, widths[level] // tile, add, 0)

    def kept(c, level):
        base = block_of(c)[1]
        return pl.ds(at_multiple(base + offsets[level], widths[level]), widths[level])

    def gather_start(c, level):
        region = total.at[block_of(c)[0], pl.ds(0, height(c)), kept(c, level)]
        send(c, bits + level, region, region, (partner[level], shard))

    def push(block, start):
        def step(i, carry):
            cols = pl.ds(at_multiple(start + i * TILE, TILE), TILE)
            summed_grad = wide(total[block, :, cols])
            moment_wide = momentum_decay * wide(moment[block, :, cols]) + summed_grad
            moment[block, :, cols] = moment_wide.astype(jnp.bfloat16)
            pushed[block, 0:rows, cols] = (
                summed_grad + momentum_decay * moment_wide
            ).astype(jnp.bfloat16)
            return carry

        lax.fori_loop(0, widths[0] // TILE, step, 0)

    stores = []

    def store(src, dst, slot):
        copy = pltpu.make_async_copy(src, dst, local_sem.at[slot])
        copy.start()
        stores.append(copy)

    def group_stage(c, s):
        block, base = block_of(c)
        if s == 0:
            scatter_start(c, 0)
        elif s < bits:
            scatter_finish(c, s - 1)
            scatter_start(c, s)
        elif s == bits:
            scatter_finish(c, bits - 1)
            gather_start(c, bits - 1)
        elif s < 2 * bits:
            level = 2 * bits - s
            started[(c, bits + level)].wait_recv()
            gather_start(c, level - 1)
            if level == 1 and block < MATS:
                ready("moment")
                push(block, base + offsets[0])
                send(
                    c,
                    2 * bits,
                    pushed.at[block, pl.ds(0, rows), kept(c, 0)],
                    pushed.at[block, pl.ds(rows, rows), kept(c, 0)],
                    (me, other_shard),
                )
        else:
            started[(c, bits)].wait_recv()
            if block < MATS:
                push(block, base + widths[0] - offsets[0])
                if c % PIECES == PIECES - 1:
                    store(moment.at[block], new_moment_hbm.at[block], 3 + MATS + block)
            else:
                cols = pl.ds(base, width)
                small_out[:, cols] = total[block, 0:SMALL_ROWS, cols]

    def shard_stage(c, s):
        block, base = block_of(c)
        if s == 0:
            started[(c, 2 * bits)].wait_recv()
            region = pushed.at[block, pl.ds(rows, rows), kept(c, 0)]
            send(c, 2 * bits + 1, region, region, (partner[0], shard))
        else:
            started[(c, 2 * bits + 1)].wait_recv()
            piece = pushed[block, :, base : base + width]
            value = lax.dot_general(
                piece, piece, (((1,), (1,)), ((), ())), preferred_element_type=jnp.float32
            )
            gram0[block] = value if c % PIECES == 0 else gram0[block] + value

    def narrow_dot(left, right):
        return jnp.dot(
            left.astype(jnp.bfloat16),
            right.astype(jnp.bfloat16),
            preferred_element_type=jnp.float32,
        )

    def full_sum(value):
        return jnp.sum(jnp.sum(value, axis=1, keepdims=True), axis=0, keepdims=True)

    muon_scale = 0.2 * math.sqrt(max(HEAD, D))
    batch = MATS // 2

    def solve_stage(half, s):
        members = range(half * batch, (half + 1) * batch)
        if s < NS_ITERS:
            here = lax.broadcasted_iota(jnp.int32, (HEAD, HEAD), 0)
            there = lax.broadcasted_iota(jnp.int32, (HEAD, HEAD), 1)
            eye = jnp.where(here == there, 1.0, 0.0).astype(jnp.float32)
            grams, scales = [], []
            for c in members:
                if s == 0 or s == NS_ITERS - 1:
                    scale = 1.0 / (jnp.sqrt(full_sum(gram0[c] * eye)) + norm_epsilon)
                    scales.append(scale)
                grams.append(gram0[c] * scale * scale if s == 0 else gram[c])
            squares = [narrow_dot(g, g) for g in grams]
            blends = [
                quintic_a * eye + quintic_b * g + quintic_c * q for g, q in zip(grams, squares)
            ]
            if s == 0:
                products = blends
            else:
                products = [narrow_dot(b, product[c]) for b, c in zip(blends, members)]
            if s < NS_ITERS - 1:
                halves = [narrow_dot(b, g) for b, g in zip(blends, grams)]
                grams = [narrow_dot(h, b) for h, b in zip(halves, blends)]
                for c, p, g in zip(members, products, grams):
                    product[c] = p
                    gram[c] = g
            else:
                for c, p, scale in zip(members, products, scales):
                    scaled = p * scale
                    energy = full_sum(scaled * gram0[c]) / (HEAD * math.sqrt(D))
                    energy_out[pl.ds(c, 1), :] = jnp.broadcast_to(energy, (1, 128))
                    polynomial[c] = scaled[0:rows].astype(jnp.bfloat16)
            return
        c = members[s - NS_ITERS]
        ready("weight")

        def update(i, carry):
            cols = pl.ds(at_multiple(i * TILE, TILE), TILE)
            ortho = jnp.dot(
                polynomial[c], pushed[c, :, cols], preferred_element_type=jnp.float32
            ).astype(jnp.bfloat16)
            weight[c, :, cols] = (
                wide(weight[c, :, cols]) * (1.0 - muon_rate * weight_decay)
                - muon_rate * muon_scale * wide(ortho)
            ).astype(jnp.bfloat16)
            return carry

        lax.fori_loop(0, weight.shape[2] // TILE, update, 0)
        store(weight.at[c], new_weight_hbm.at[c], 3 + 2 * MATS + c)

    count = [0] * (2 * chains + 2)
    for code in ORDER:
        s = count[code]
        count[code] += 1
        if code < chains:
            group_stage(code, s)
        elif code < 2 * chains:
            shard_stage(code - chains, s)
        else:
            solve_stage(code - 2 * chains, s)
    for copy in started.values():
        copy.wait_send()
    for copy in stores:
        copy.wait()


def finish_kernel(
    owners,
    small,
    energy,
    weight_hbm,
    moment_hbm,
    *refs,
):
    adam, outs = refs[:9], refs[9:-1]
    sem = refs[-1]
    new_weight, new_moment, owner_sums = outs[:3]
    copies = []
    for b in range(MATS):
        for slot, src, dst in ((0, weight_hbm, new_weight), (1, moment_hbm, new_moment)):
            copy = pltpu.make_async_copy(src.at[b], dst.at[b], sem.at[slot, b])
            copy.start()
            copies.append(copy)
    shard = lax.axis_index("shard")
    lane = lax.broadcasted_iota(jnp.int32, (1, 128), 1)
    row = jnp.zeros((1, 128), jnp.float32)
    for i in range(MATS):
        slot = owners[i] * HALF_MATS
        for j in range(i):
            slot = slot + jnp.where(owners[j] == owners[i], 1, 0)
        row = row + jnp.where(lane == slot - shard * HALF_MATS, energy[i : i + 1, :], 0.0)
    owner_sums[...] = row[:, 0:HALF_MATS]
    emb_rows = adam[0].shape[0]
    gains = adam[3].shape[1]
    heads = adam[6].shape[1]

    def emb_step(i, carry):
        cols = pl.ds(pl.multiple_of(i * TILE, TILE), TILE)
        results = adamw(
            adam[0][:, cols], wide(small[0:emb_rows, cols]), adam[1][:, cols], adam[2][:, cols]
        )
        for ref, result in zip(outs[3:6], results):
            ref[:, cols] = result
        return carry

    lax.fori_loop(0, adam[0].shape[1] // TILE, emb_step, 0)
    extra = wide(small[emb_rows:SMALL_ROWS, 0 : gains + heads])
    for k, cols in ((1, slice(0, gains)), (2, slice(gains, gains + heads))):
        weight, first, second = adam[3 * k : 3 * k + 3]
        results = adamw(weight[...], extra[0:2, cols], first[...], second[...])
        for ref, result in zip(outs[3 + 3 * k : 6 + 3 * k], results):
            ref[...] = result
    for copy in copies:
        copy.wait()


def linked_device(
    groups,
    owners,
    mat_weight,
    mat_grad,
    head_block_momentum,
    emb_weight,
    emb_grad,
    emb_first,
    emb_second,
    norm_weight,
    norm_grad,
    norm_first,
    norm_second,
    qk_weight,
    qk_grad,
    qk_first,
    qk_second,
):
    bits = groups.bit_length() - 1
    blocks, rows, width = mat_weight.shape
    levels = [width // PIECES >> (level + 1) for level in range(bits)]
    chains = (blocks + 1) * PIECES
    in_vmem = pl.BlockSpec(memory_space=pltpu.VMEM)
    anywhere = pl.BlockSpec(memory_space=pl.ANY)
    block_shape = (blocks, rows, width)
    new_weight, new_moment, small_sum, energy = pl.pallas_call(
        functools.partial(linked_kernel, bits),
        out_shape=(
            jax.ShapeDtypeStruct(block_shape, jnp.bfloat16),
            jax.ShapeDtypeStruct(block_shape, jnp.bfloat16),
            jax.ShapeDtypeStruct((SMALL_ROWS, width), jnp.bfloat16),
            jax.ShapeDtypeStruct((8, 128), jnp.float32),
        ),
        in_specs=[in_vmem] * 2 + [anywhere] * 4,
        out_specs=(anywhere, anywhere, in_vmem, in_vmem),
        scratch_shapes=[
            pltpu.VMEM(block_shape, jnp.bfloat16),
            pltpu.VMEM(block_shape, jnp.bfloat16),
            pltpu.VMEM(block_shape, jnp.bfloat16),
            pltpu.VMEM((SMALL_ROWS, width), jnp.bfloat16),
            pltpu.VMEM((blocks + 1, rows, width), jnp.bfloat16),
            pltpu.VMEM((blocks, 2 * rows, width), jnp.bfloat16),
            pltpu.VMEM((blocks, HEAD, HEAD), jnp.float32),
            pltpu.VMEM((blocks, HEAD, HEAD), jnp.float32),
            pltpu.VMEM((blocks, HEAD, HEAD), jnp.float32),
            pltpu.VMEM((blocks, rows, HEAD), jnp.bfloat16),
            pltpu.SemaphoreType.DMA((3 + 3 * blocks,)),
            pltpu.SemaphoreType.DMA((chains, 2 * bits + 2)),
            pltpu.SemaphoreType.DMA((chains, 2 * bits + 2)),
        ]
        + [pltpu.VMEM((chains, rows, part), jnp.bfloat16) for part in levels]
        + [pltpu.VMEM((chains, rows, part), jnp.bfloat16) for part in levels[:-1]],
        compiler_params=pltpu.CompilerParams(
            collective_id=0, has_side_effects=True, vmem_limit_bytes=56 * 1024 * 1024
        ),
    )(norm_grad[0], qk_grad[0], mat_grad[0], emb_grad[0], head_block_momentum, mat_weight)
    adam = (
        emb_weight,
        emb_first,
        emb_second,
        norm_weight,
        norm_first,
        norm_second,
        qk_weight,
        qk_first,
        qk_second,
    )
    return pl.pallas_call(
        finish_kernel,
        out_shape=(
            jax.ShapeDtypeStruct(block_shape, jnp.bfloat16),
            jax.ShapeDtypeStruct(block_shape, jnp.bfloat16),
            jax.ShapeDtypeStruct((1, HALF_MATS), jnp.float32),
        )
        + tuple(jax.ShapeDtypeStruct(a.shape, a.dtype) for a in adam),
        in_specs=[pl.BlockSpec(memory_space=pltpu.SMEM), in_vmem, in_vmem, anywhere, anywhere]
        + [in_vmem] * 9,
        out_specs=(anywhere, anywhere) + (in_vmem,) * 10,
        scratch_shapes=[pltpu.SemaphoreType.DMA((2, blocks))],
        compiler_params=pltpu.CompilerParams(vmem_limit_bytes=32 * 1024 * 1024),
    )(owners, small_sum, energy, new_weight, new_moment, *adam)


def solution(mesh):
    plan = on_device
    if links_fit(mesh.shape["group"], mesh.shape["shard"]):
        plan = functools.partial(linked_device, mesh.shape["group"])
    placed = (
        P(),
        P(None, "shard", None),
        P("group", None, "shard", None),
        P(None, "shard", None),
        P("shard", None),
        P("group", "shard", None),
        P("shard", None),
        P("shard", None),
        P(None, "shard"),
        P("group", None, "shard"),
        P(None, "shard"),
        P(None, "shard"),
        P(),
        P("group", None, None),
        P(),
        P(),
    )
    return jax.shard_map(
        plan,
        mesh=mesh,
        in_specs=placed,
        out_specs=(
            P(None, "shard", None),
            P(None, "shard", None),
            P("shard", None),
            P("shard", None),
            P("shard", None),
            P("shard", None),
            P(None, "shard"),
            P(None, "shard"),
            P(None, "shard"),
            P(),
            P(),
            P(),
        ),
        check_vma=False,
    )
```

time: 102 us -> 88 us (0.86); the launches traced: 100 us -> 87.7 us
  other arithmetic: 8.15 us -> 0 us
  Pallas kernels: 85.8 us -> 81.4 us
    pallas_call x1, Pallas kernels: 85.8 us -> 77 us  [linked_device(): pl.pallas_call(functools.partial(linked_kernel, bits), out_shape=(jax.Sha...]
    convert_element_type x4 -> x0, other arithmetic: 4.81 us -> none  [the longest x3 3.76 us: adamw(): (wide_weight - adam_rate * stepped).astype(jnp.bfloat16)]
    pallas_call x0 -> x1, Pallas kernels: none -> 4.36 us  [linked_device(): pl.pallas_call(finish_kernel, out_shape=(jax.ShapeDtypeStruct(block_shape...]
    concatenate x2 -> x0, other arithmetic: 2.46 us -> none  [the longest x1 1.72 us: linked_device(): small = jnp.concatenate([emb_grad[0], extra], axis=0)]
    unnamed x22 -> x28, local copies, waits for them, and re-layouts: 4.74 us -> 5.48 us
where the time goes in v2:
time: 88 us; the launch traced here: 87.7 us
  Pallas kernels  81.4 us (93%)
  local copies, waits for them, and re-layouts  5.48 us (6%)
    pallas_call x1, Pallas kernels, linked_device(): pl.pallas_call(functools.partial(linked_kernel, bits), out_shape=(jax.Sha...  77 us
    unnamed x28, local copies, waits for them, and re-layouts  5.48 us
    pallas_call x1, Pallas kernels, linked_device(): pl.pallas_call(finish_kernel, out_shape=(jax.ShapeDtypeStruct(block_shape...  4.36 us

profile of v2, /device:TPU:0, one launch (start us, length us, event | category | flops | bytes accessed | tf_op | source)
XLA Modules:
  0.0 87.7 jit_solution(10307346079437069619)
XLA Ops:
  0.7 0.0 copy-start.2
  0.7 0.0 copy-start.3
  0.7 0.0 copy-start.5
  0.7 0.0 copy-start.6
  0.7 0.0 copy-start.7
  0.7 0.0 copy-start.8
  0.7 0.0 copy-start.10
  0.7 0.0 copy-start.11
  0.7 0.0 copy-start.12
  0.7 0.0 copy-start.13
  0.8 77.0 %shard_map.247 = (bf16[6,64,4096]{2,1,0:T(8,128)(2,1)}, bf16[6,64,4096]{2,1,0:T(8,128)(2,1)}, bf16[48,4096]{1,0:T(8,128)(2,1)}, f32[8,128]{1,0:T(8,128)}) custom-call(bf16[2,2048]{1,0:T(2,128)(2,1)} %bitcast.6, bf16[2,128]{1,0:T(2,128)(2,1)} %bitcast.7, bf16[6,64,4096]{2,1,0:T(8,128)(2,1)} %bitcast.4, bf16[32,4096]{1,0:T(8,128)(2,1)} %bitcast.5, ...), custom_call_target="tpu_custom_call" | custom-call | tf_op jit(solution)/shard_map/pallas_call | solution.py:545
  77.8 0.0 copy-done.2
  77.8 0.0 copy-done.3
  77.8 0.0 copy-done.5
  77.8 0.0 copy-done.6
  77.8 0.0 copy-done.7
  77.8 0.0 copy-done.8
  77.9 0.0 copy-done.10
  77.9 0.0 copy-done.11
  77.9 0.0 copy-done.12
  77.9 0.0 copy-done.13
  77.9 0.0 copy-start
  77.9 1.9 %copy-done = bf16[6,64,4096]{2,1,0:T(8,128)(2,1)S(1)} copy-done((bf16[6,64,4096]{2,1,0:T(8,128)(2,1)S(1)}, bf16[6,64,4096]{2,1,0:T(8,128)(2,1)}, u32[]{:S(2)}) %copy-start) | copy-done | bytes 3145752
  79.8 0.0 copy-start.1
  79.8 1.9 %copy-done.1 = bf16[6,64,4096]{2,1,0:T(8,128)(2,1)S(1)} copy-done((bf16[6,64,4096]{2,1,0:T(8,128)(2,1)S(1)}, bf16[6,64,4096]{2,1,0:T(8,128)(2,1)}, u32[]{:S(2)}) %copy-start.1) | copy-done | bytes 3145752
  81.7 0.0 copy-start.4
  81.7 1.0 %copy-done.4 = bf16[48,4096]{1,0:T(8,128)(2,1)S(1)} copy-done((bf16[48,4096]{1,0:T(8,128)(2,1)S(1)}, bf16[48,4096]{1,0:T(8,128)(2,1)}, u32[]{:S(2)}) %copy-start.4) | copy-done | bytes 393240
  82.7 0.0 copy-start.9
  82.7 0.7 copy-done.9
  83.3 4.4 %shard_map.248 = (bf16[6,64,4096]{2,1,0:T(8,128)(2,1)}, bf16[6,64,4096]{2,1,0:T(8,128)(2,1)}, f32[1,3]{1,0:T(1,128)}, bf16[32,4096]{1,0:T(8,128)(2,1)}, f32[32,4...) custom-call(s32[6]{0:T(128)S(1)} %copy-done.12, ...), custom_call_target="tpu_custom_call" | custom-call | tf_op jit(solution)/shard_map/pallas_call | solution.py:587
Async XLA Ops:
  0.7 77.1 %copy-start.2 = (f32[32,4096]{1,0:T(8,128)S(1)}, f32[32,4096]{1,0:T(8,128)}, u32[]{:S(2)}) copy-start(f32[32,4096]{1,0:T(8,128)} %refs_1_.1) | copy-start | bytes 1572868
  0.7 77.1 %copy-start.3 = (f32[32,4096]{1,0:T(8,128)S(1)}, f32[32,4096]{1,0:T(8,128)}, u32[]{:S(2)}) copy-start(f32[32,4096]{1,0:T(8,128)} %refs_2_.1) | copy-start | bytes 1572868
  0.7 77.1 %copy-start.5 = (bf16[32,4096]{1,0:T(8,128)(2,1)S(1)}, bf16[32,4096]{1,0:T(8,128)(2,1)}, u32[]{:S(2)}) copy-start(bf16[32,4096]{1,0:T(8,128)(2,1)} %refs_0_.1) | copy-start | bytes 786436
  0.7 77.1 %copy-start.6 = (f32[2,2048]{1,0:T(2,128)S(1)}, f32[2,2048]{1,0:T(2,128)}, u32[]{:S(2)}) copy-start(f32[2,2048]{1,0:T(2,128)} %refs_4_.1) | copy-start | bytes 49156
  0.7 77.1 %copy-start.7 = (f32[2,2048]{1,0:T(2,128)S(1)}, f32[2,2048]{1,0:T(2,128)}, u32[]{:S(2)}) copy-start(f32[2,2048]{1,0:T(2,128)} %refs_5_.1) | copy-start | bytes 49156
  0.7 77.1 %copy-start.8 = (bf16[2,2048]{1,0:T(2,128)(2,1)S(1)}, bf16[2,2048]{1,0:T(2,128)(2,1)}, u32[]{:S(2)}) copy-start(bf16[2,2048]{1,0:T(2,128)(2,1)} %refs_3_.1) | copy-start | bytes 24580
  0.7 77.1 %copy-start.10 = (f32[2,128]{1,0:T(2,128)S(1)}, f32[2,128]{1,0:T(2,128)}, u32[]{:S(2)}) copy-start(f32[2,128]{1,0:T(2,128)} %refs_7_.1) | copy-start | bytes 3076
  0.7 77.1 %copy-start.11 = (f32[2,128]{1,0:T(2,128)S(1)}, f32[2,128]{1,0:T(2,128)}, u32[]{:S(2)}) copy-start(f32[2,128]{1,0:T(2,128)} %refs_8_.1) | copy-start | bytes 3076
  0.7 77.1 %copy-start.12 = (s32[6]{0:T(128)S(1)}, s32[6]{0:T(128)}, u32[]{:S(2)}) copy-start(s32[6]{0:T(128)} %owners.1) | copy-start | bytes 76
  0.7 77.1 %copy-start.13 = (bf16[2,128]{1,0:T(2,128)(2,1)S(1)}, bf16[2,128]{1,0:T(2,128)(2,1)}, u32[]{:S(2)}) copy-start(bf16[2,128]{1,0:T(2,128)(2,1)} %refs_6_.1) | copy-start | bytes 1540
  77.9 1.9 %copy-start = (bf16[6,64,4096]{2,1,0:T(8,128)(2,1)S(1)}, bf16[6,64,4096]{2,1,0:T(8,128)(2,1)}, u32[]{:S(2)}) copy-start(bf16[6,64,4096]{2,1,0:T(8,128)(2,1)} %get-tuple-element.18.weight_hbm) | copy-start | bytes 9437188
  79.8 1.9 %copy-start.1 = (bf16[6,64,4096]{2,1,0:T(8,128)(2,1)S(1)}, bf16[6,64,4096]{2,1,0:T(8,128)(2,1)}, u32[]{:S(2)}) copy-start(bf16[6,64,4096]{2,1,0:T(8,128)(2,1)} %get-tuple-element.19.moment_hbm) | copy-start | bytes 9437188
  81.7 1.0 %copy-start.4 = (bf16[48,4096]{1,0:T(8,128)(2,1)S(1)}, bf16[48,4096]{1,0:T(8,128)(2,1)}, u32[]{:S(2)}) copy-start(bf16[48,4096]{1,0:T(8,128)(2,1)} %get-tuple-element.16.small) | copy-start | bytes 1179652
  82.7 0.7 copy-start.9

commit v3 on v2

--- a/solution.py
+++ b/solution.py
@@ -1,4 +1,3 @@
-import functools
 import math
 
 import jax
@@ -148,18 +147,21 @@
 TILE = 512
 PIECES = 2
 ORDER = (
-    0, 1, 2, 3, 4, 5, 6, 7, 8, 9, 10, 11, 12, 13, 0, 1, 2, 3, 4, 5, 6, 7, 0, 8, 9, 1, 10, 11,
-    2, 0, 12, 13, 1, 3, 2, 4, 0, 1, 5, 3, 2, 6, 4, 0, 7, 1, 5, 3, 8, 2, 6, 9, 4, 0, 10, 7, 1,
-    11, 5, 3, 12, 8, 13, 2, 6, 0, 9, 4, 1, 10, 0, 7, 2, 5, 11, 1, 3, 12, 14, 2, 8, 13, 6, 9,
-    14, 3, 15, 4, 10, 7, 5, 3, 15, 16, 8, 11, 4, 12, 13, 6, 5, 16, 17, 4, 7, 9, 10, 5, 6, 8,
-    11, 17, 18, 12, 13, 9, 7, 6, 10, 11, 18, 8, 19, 7, 9, 12, 13, 8, 10, 19, 20, 11, 9, 10,
-    12, 28, 13, 20, 21, 11, 12, 28, 22, 13, 21, 28, 28, 22, 23, 28, 28, 28, 23, 24, 28, 25,
-    24, 25, 29, 29, 29, 29, 29, 29, 29, 29,
+    0, 1, 2, 3, 4, 5, 6, 7, 8, 9, 10, 11, 12, 13, 0, 1, 2, 3, 4, 5, 6, 7, 0, 1, 2, 3, 0, 4, 1,
+    5, 2, 6, 3, 7, 0, 8, 4, 1, 9, 5, 0, 2, 10, 8, 6, 1, 0, 3, 11, 9, 7, 2, 1, 4, 12, 10, 14,
+    5, 13, 3, 2, 8, 11, 15, 14, 4, 3, 6, 9, 12, 16, 5, 7, 15, 4, 10, 13, 17, 8, 16, 6, 5, 7,
+    11, 18, 9, 17, 19, 12, 8, 6, 7, 10, 18, 13, 19, 9, 8, 11, 12, 20, 28, 21, 28, 10, 9, 13,
+    20, 22, 28, 11, 12, 10, 21, 23, 28, 13, 22, 11, 12, 24, 28, 23, 13, 28, 25, 28, 24, 28,
+    25, 29, 29, 29, 29, 29, 29, 29, 29,
 )
+BATCHES = ((0, 1, 2), (3, 4, 5))
+HALVINGS = 2
+LINE = 4
+GATHER, EXCHANGE, RELAY, SLOTS = 5, 10, 11, 12
 
 
 def links_fit(groups, shards):
-    return groups == 16 and shards == 2
+    return groups == LINE << HALVINGS and shards == 2
 
 
 def wide(value):
@@ -167,7 +169,6 @@
 
 
 def linked_kernel(
-    bits,
     norm_ref,
     qk_ref,
     grad_hbm,
@@ -193,24 +194,28 @@
     recv_sem,
     *levels,
 ):
-    landed, summed = levels[:bits], levels[bits:]
+    landed, line_landed, summed = levels[:HALVINGS], levels[HALVINGS], levels[HALVINGS + 1 :]
     rows, width = grad.shape[1], grad.shape[2] // PIECES
     chains = (MATS + 1) * PIECES
-    widths = [width >> (level + 1) for level in range(bits)]
+    widths = [width >> (level + 1) for level in range(HALVINGS)]
+    piece = widths[-1] // LINE
     me = lax.axis_index("group")
     shard = lax.axis_index("shard")
-    digit = [lax.rem(lax.div(me, 1 << b), 2) for b in range(bits)]
-    partner = [me + (1 << b) * (1 - 2 * digit[b]) for b in range(bits)]
+    digit = [lax.rem(lax.div(me, 1 << b), 2) for b in range(HALVINGS)]
+    partner = [me + (1 << b) * (1 - 2 * digit[b]) for b in range(HALVINGS)]
+    spot = lax.div(me, 1 << HALVINGS)
+    peer_spot = [lax.rem(spot + step, LINE) for step in range(1, LINE)]
+    peers = [me + (there - spot) * (1 << HALVINGS) for there in peer_spot]
     other_shard = 1 - shard
     offsets = []
-    for level in range(bits):
+    for level in range(HALVINGS):
         before = offsets[-1] if offsets else 0
         offsets.append(before + digit[level] * widths[level])
 
     barrier = pltpu.get_barrier_semaphore()
-    for b in range(bits):
+    for device in partner + peers:
         pl.semaphore_signal(
-            barrier, inc=1, device_id=(partner[b], shard), device_id_type=pl.DeviceIdType.MESH
+            barrier, inc=1, device_id=(device, shard), device_id_type=pl.DeviceIdType.MESH
         )
     pl.semaphore_signal(
         barrier, inc=1, device_id=(me, other_shard), device_id_type=pl.DeviceIdType.MESH
@@ -234,7 +239,7 @@
             jnp.bfloat16
         )
         place += part.shape[1]
-    pl.semaphore_wait(barrier, bits + 1)
+    pl.semaphore_wait(barrier, len(partner) + len(peers) + 1)
 
     def ready(key):
         if key in loads:
@@ -293,17 +298,14 @@
         keep = keep + digit[level] * widths[level]
         tile = min(TILE, widths[level])
         arrived = landed[level].at[c, pl.ds(0, height(c))]
-        if level == bits - 1:
-            target, place = total.at[block, pl.ds(0, height(c))], base + offsets[level]
-        else:
-            target, place = summed[level].at[c, pl.ds(0, height(c))], 0
+        target = summed[level].at[c, pl.ds(0, height(c))]
 
         def add(i, carry):
             at = at_multiple(i * tile, tile)
             value = wide(arrived[:, pl.ds(at, tile)]) + wide(
                 mine[:, pl.ds(at_multiple(keep + at, tile), tile)]
             )
-            target[:, pl.ds(at_multiple(place + at, tile), tile)] = value.astype(jnp.bfloat16)
+            target[:, pl.ds(at, tile)] = value.astype(jnp.bfloat16)
             return carry
 
         if widths[level] == tile:
@@ -315,9 +317,34 @@
         base = block_of(c)[1]
         return pl.ds(at_multiple(base + offsets[level], widths[level]), widths[level])
 
+    def line_scatter(c):
+        for k in range(LINE - 1):
+            start = at_multiple(peer_spot[k] * piece, piece)
+            send(
+                c,
+                HALVINGS + k,
+                summed[-1].at[c, pl.ds(0, height(c)), pl.ds(start, piece)],
+                line_landed.at[c, k, pl.ds(0, height(c))],
+                (peers[k], shard),
+            )
+
+    def line_gather(c):
+        block, base = block_of(c)
+        value = wide(
+            summed[-1][c, 0 : height(c), pl.ds(at_multiple(spot * piece, piece), piece)]
+        )
+        for k in range(LINE - 1):
+            started[(c, HALVINGS + k)].wait_recv()
+            value = value + wide(line_landed[c, k, 0 : height(c)])
+        start = at_multiple(base + offsets[-1] + spot * piece, piece)
+        region = total.at[block, pl.ds(0, height(c)), pl.ds(start, piece)]
+        region[...] = value.astype(jnp.bfloat16)
+        for k in range(LINE - 1):
+            send(c, GATHER + k, region, region, (peers[k], shard))
+
     def gather_start(c, level):
         region = total.at[block_of(c)[0], pl.ds(0, height(c)), kept(c, level)]
-        send(c, bits + level, region, region, (partner[level], shard))
+        send(c, EXCHANGE - 1 - level, region, region, (partner[level], shard))
 
     def push(block, start):
         def step(i, carry):
@@ -343,28 +370,33 @@
         block, base = block_of(c)
         if s == 0:
             scatter_start(c, 0)
-        elif s < bits:
-            scatter_finish(c, s - 1)
-            scatter_start(c, s)
-        elif s == bits:
-            scatter_finish(c, bits - 1)
-            gather_start(c, bits - 1)
-        elif s < 2 * bits:
-            level = 2 * bits - s
-            started[(c, bits + level)].wait_recv()
-            gather_start(c, level - 1)
-            if level == 1 and block < MATS:
+        elif s == 1:
+            scatter_finish(c, 0)
+            scatter_start(c, 1)
+        elif s == 2:
+            scatter_finish(c, 1)
+            line_scatter(c)
+        elif s == 3:
+            line_gather(c)
+        elif s == 4:
+            for k in range(LINE - 1):
+                started[(c, GATHER + k)].wait_recv()
+            gather_start(c, 1)
+        elif s == 5:
+            started[(c, EXCHANGE - 2)].wait_recv()
+            gather_start(c, 0)
+            if block < MATS:
                 ready("moment")
                 push(block, base + offsets[0])
                 send(
                     c,
-                    2 * bits,
+                    EXCHANGE,
                     pushed.at[block, pl.ds(0, rows), kept(c, 0)],
                     pushed.at[block, pl.ds(rows, rows), kept(c, 0)],
                     (me, other_shard),
                 )
         else:
-            started[(c, bits)].wait_recv()
+            started[(c, EXCHANGE - 1)].wait_recv()
             if block < MATS:
                 push(block, base + widths[0] - offsets[0])
                 if c % PIECES == PIECES - 1:
@@ -376,14 +408,14 @@
     def shard_stage(c, s):
         block, base = block_of(c)
         if s == 0:
-            started[(c, 2 * bits)].wait_recv()
+            started[(c, EXCHANGE)].wait_recv()
             region = pushed.at[block, pl.ds(rows, rows), kept(c, 0)]
-            send(c, 2 * bits + 1, region, region, (partner[0], shard))
+            send(c, RELAY, region, region, (partner[0], shard))
         else:
-            started[(c, 2 * bits + 1)].wait_recv()
-            piece = pushed[block, :, base : base + width]
+            started[(c, RELAY)].wait_recv()
+            part = pushed[block, :, base : base + width]
             value = lax.dot_general(
-                piece, piece, (((1,), (1,)), ((), ())), preferred_element_type=jnp.float32
+                part, part, (((1,), (1,)), ((), ())), preferred_element_type=jnp.float32
             )
             gram0[block] = value if c % PIECES == 0 else gram0[block] + value
 
@@ -398,10 +430,9 @@
         return jnp.sum(jnp.sum(value, axis=1, keepdims=True), axis=0, keepdims=True)
 
     muon_scale = 0.2 * math.sqrt(max(HEAD, D))
-    batch = MATS // 2
-
-    def solve_stage(half, s):
-        members = range(half * batch, (half + 1) * batch)
+
+    def solve_stage(batch, s):
+        members = BATCHES[batch]
         if s < NS_ITERS:
             here = lax.broadcasted_iota(jnp.int32, (HEAD, HEAD), 0)
             there = lax.broadcasted_iota(jnp.int32, (HEAD, HEAD), 1)
@@ -450,7 +481,7 @@
         lax.fori_loop(0, weight.shape[2] // TILE, update, 0)
         store(weight.at[c], new_weight_hbm.at[c], 3 + 2 * MATS + c)
 
-    count = [0] * (2 * chains + 2)
+    count = [0] * (2 * chains + len(BATCHES))
     for code in ORDER:
         s = count[code]
         count[code] += 1
@@ -517,7 +548,6 @@
 
 
 def linked_device(
-    groups,
     owners,
     mat_weight,
     mat_grad,
@@ -535,15 +565,14 @@
     qk_first,
     qk_second,
 ):
-    bits = groups.bit_length() - 1
     blocks, rows, width = mat_weight.shape
-    levels = [width // PIECES >> (level + 1) for level in range(bits)]
+    levels = [width // PIECES >> (level + 1) for level in range(HALVINGS)]
     chains = (blocks + 1) * PIECES
     in_vmem = pl.BlockSpec(memory_space=pltpu.VMEM)
     anywhere = pl.BlockSpec(memory_space=pl.ANY)
     block_shape = (blocks, rows, width)
     new_weight, new_moment, small_sum, energy = pl.pallas_call(
-        functools.partial(linked_kernel, bits),
+        linked_kernel,
         out_shape=(
             jax.ShapeDtypeStruct(block_shape, jnp.bfloat16),
             jax.ShapeDtypeStruct(block_shape, jnp.bfloat16),
@@ -564,11 +593,12 @@
             pltpu.VMEM((blocks, HEAD, HEAD), jnp.float32),
             pltpu.VMEM((blocks, rows, HEAD), jnp.bfloat16),
             pltpu.SemaphoreType.DMA((3 + 3 * blocks,)),
-            pltpu.SemaphoreType.DMA((chains, 2 * bits + 2)),
-            pltpu.SemaphoreType.DMA((chains, 2 * bits + 2)),
+            pltpu.SemaphoreType.DMA((chains, SLOTS)),
+            pltpu.SemaphoreType.DMA((chains, SLOTS)),
         ]
         + [pltpu.VMEM((chains, rows, part), jnp.bfloat16) for part in levels]
-        + [pltpu.VMEM((chains, rows, part), jnp.bfloat16) for part in levels[:-1]],
+        + [pltpu.VMEM((chains, LINE - 1, rows, levels[-1] // LINE), jnp.bfloat16)]
+        + [pltpu.VMEM((chains, rows, part), jnp.bfloat16) for part in levels],
         compiler_params=pltpu.CompilerParams(
             collective_id=0, has_side_effects=True, vmem_limit_bytes=56 * 1024 * 1024
         ),
@@ -592,18 +622,19 @@
             jax.ShapeDtypeStruct((1, HALF_MATS), jnp.float32),
         )
         + tuple(jax.ShapeDtypeStruct(a.shape, a.dtype) for a in adam),
-        in_specs=[pl.BlockSpec(memory_space=pltpu.SMEM), in_vmem, in_vmem, anywhere, anywhere]
+        in_specs=[pl.BlockSpec(memory_space=pltpu.SMEM), in_vmem, in_vmem]
+        + [anywhere] * 2
         + [in_vmem] * 9,
         out_specs=(anywhere, anywhere) + (in_vmem,) * 10,
         scratch_shapes=[pltpu.SemaphoreType.DMA((2, blocks))],
-        compiler_params=pltpu.CompilerParams(vmem_limit_bytes=32 * 1024 * 1024),
+        compiler_params=pltpu.CompilerParams(vmem_limit_bytes=61 * 1024 * 1024),
     )(owners, small_sum, energy, new_weight, new_moment, *adam)
 
 
 def solution(mesh):
     plan = on_device
     if links_fit(mesh.shape["group"], mesh.shape["shard"]):
-        plan = functools.partial(linked_device, mesh.shape["group"])
+        plan = linked_device
     placed = (
         P(),
         P(None, "shard", None),

time: 88 us -> 272 us (3.09)
  Pallas kernels: 81.4 us -> 271 us
  local copies, waits for them, and re-layouts: 5.48 us -> 0 us
    pallas_call x1, Pallas kernels: 4.36 us -> 194 us  [linked_device(): pl.pallas_call(finish_kernel, out_shape=(jax.ShapeDtypeStruct(block_shape...]
    unnamed x28 -> x0, local copies, waits for them, and re-layouts: 5.48 us -> none
where the time goes in v3:
time: 272 us; the launch traced here: 271 us
  Pallas kernels  271 us (100%)
    pallas_call x1, Pallas kernels, linked_device(): pl.pallas_call(finish_kernel, out_shape=(jax.ShapeDtypeStruct(block_shape...  194 us
    pallas_call x1, Pallas kernels, linked_device(): pl.pallas_call(linked_kernel, out_shape=(jax.ShapeDtypeStruct(block_shape...  76.1 us

profile of v3, /device:TPU:0, one launch (start us, length us, event | category | flops | bytes accessed | tf_op | source)
XLA Modules:
  0.0 271.2 jit_solution(7527530955831849590)
XLA Ops:
  0.6 76.1 %shard_map.247 = (bf16[6,64,4096]{2,1,0:T(8,128)(2,1)}, bf16[6,64,4096]{2,1,0:T(8,128)(2,1)}, bf16[48,4096]{1,0:T(8,128)(2,1)}, f32[8,128]{1,0:T(8,128)}) custom-call(bf16[2,2048]{1,0:T(2,128)(2,1)} %bitcast.6, bf16[2,128]{1,0:T(2,128)(2,1)} %bitcast.7, bf16[6,64,4096]{2,1,0:T(8,128)(2,1)} %bitcast.4, bf16[32,4096]{1,0:T(8,128)(2,1)} %bitcast.5, ...), custom_call_target="tpu_custom_call" | custom-call | tf_op jit(solution)/shard_map/pallas_call | solution.py:574
  76.8 194.4 %shard_map.248 = (bf16[6,64,4096]{2,1,0:T(8,128)(2,1)}, bf16[6,64,4096]{2,1,0:T(8,128)(2,1)}, f32[1,3]{1,0:T(1,128)}, bf16[32,4096]{1,0:T(8,128)(2,1)}, f32[32,4...) custom-call(s32[6]{0:T(128)} %owners.1, ...), custom_call_target="tpu_custom_call" | custom-call | tf_op jit(solution)/shard_map/pallas_call | solution.py:617

commit v4 on v3

--- a/solution.py
+++ b/solution.py
@@ -147,14 +147,14 @@
 TILE = 512
 PIECES = 2
 ORDER = (
-    0, 1, 2, 3, 4, 5, 6, 7, 8, 9, 10, 11, 12, 13, 0, 1, 2, 3, 4, 5, 6, 7, 0, 1, 2, 3, 0, 4, 1,
-    5, 2, 6, 3, 7, 0, 8, 4, 1, 9, 5, 0, 2, 10, 8, 6, 1, 0, 3, 11, 9, 7, 2, 1, 4, 12, 10, 14,
-    5, 13, 3, 2, 8, 11, 15, 14, 4, 3, 6, 9, 12, 16, 5, 7, 15, 4, 10, 13, 17, 8, 16, 6, 5, 7,
-    11, 18, 9, 17, 19, 12, 8, 6, 7, 10, 18, 13, 19, 9, 8, 11, 12, 20, 28, 21, 28, 10, 9, 13,
-    20, 22, 28, 11, 12, 10, 21, 23, 28, 13, 22, 11, 12, 24, 28, 23, 13, 28, 25, 28, 24, 28,
-    25, 29, 29, 29, 29, 29, 29, 29, 29,
+    0, 1, 2, 3, 4, 5, 6, 7, 8, 9, 10, 11, 12, 13, 0, 1, 2, 3, 4, 5, 6, 7, 0, 1, 2, 0, 3, 1, 4,
+    2, 5, 0, 8, 6, 3, 7, 1, 9, 0, 4, 2, 8, 10, 5, 0, 1, 6, 9, 3, 11, 14, 2, 1, 7, 10, 4, 12,
+    14, 15, 2, 3, 8, 5, 11, 13, 15, 16, 3, 4, 6, 9, 12, 7, 5, 16, 17, 4, 10, 13, 8, 6, 5, 17,
+    18, 7, 11, 9, 6, 12, 8, 19, 18, 7, 10, 13, 9, 8, 19, 20, 11, 28, 12, 28, 9, 10, 21, 20,
+    13, 28, 11, 28, 10, 21, 22, 12, 28, 11, 13, 28, 23, 28, 22, 12, 13, 28, 23, 24, 29, 29,
+    29, 29, 25, 29, 24, 29, 29, 25, 30, 30, 30, 30, 30, 30,
 )
-BATCHES = ((0, 1, 2), (3, 4, 5))
+BATCHES = ((0, 1, 2), (3, 4), (5,))
 HALVINGS = 2
 LINE = 4
 GATHER, EXCHANGE, RELAY, SLOTS = 5, 10, 11, 12
@@ -505,15 +505,17 @@
     moment_hbm,
     *refs,
 ):
-    adam, outs = refs[:9], refs[9:-1]
-    sem = refs[-1]
+    adam, outs = refs[:9], refs[9:-3]
+    held, load_sem, store_sem = refs[-3:]
     new_weight, new_moment, owner_sums = outs[:3]
-    copies = []
+    loads, stores = [], []
     for b in range(MATS):
         for slot, src, dst in ((0, weight_hbm, new_weight), (1, moment_hbm, new_moment)):
-            copy = pltpu.make_async_copy(src.at[b], dst.at[b], sem.at[slot, b])
-            copy.start()
-            copies.append(copy)
+            spot = held.at[slot, b]
+            loads.append(pltpu.make_async_copy(src.at[b], spot, load_sem.at[slot, b]))
+            stores.append(pltpu.make_async_copy(spot, dst.at[b], store_sem.at[slot, b]))
+    for load in loads:
+        load.start()
     shard = lax.axis_index("shard")
     lane = lax.broadcasted_iota(jnp.int32, (1, 128), 1)
     row = jnp.zeros((1, 128), jnp.float32)
@@ -536,6 +538,9 @@
             ref[:, cols] = result
         return carry
 
+    for load, store in zip(loads, stores):
+        load.wait()
+        store.start()
     lax.fori_loop(0, adam[0].shape[1] // TILE, emb_step, 0)
     extra = wide(small[emb_rows:SMALL_ROWS, 0 : gains + heads])
     for k, cols in ((1, slice(0, gains)), (2, slice(gains, gains + heads))):
@@ -543,8 +548,8 @@
         results = adamw(weight[...], extra[0:2, cols], first[...], second[...])
         for ref, result in zip(outs[3 + 3 * k : 6 + 3 * k], results):
             ref[...] = result
-    for copy in copies:
-        copy.wait()
+    for store in stores:
+        store.wait()
 
 
 def linked_device(
@@ -626,8 +631,12 @@
         + [anywhere] * 2
         + [in_vmem] * 9,
         out_specs=(anywhere, anywhere) + (in_vmem,) * 10,
-        scratch_shapes=[pltpu.SemaphoreType.DMA((2, blocks))],
-        compiler_params=pltpu.CompilerParams(vmem_limit_bytes=61 * 1024 * 1024),
+        scratch_shapes=[
+            pltpu.VMEM((2,) + block_shape, jnp.bfloat16),
+            pltpu.SemaphoreType.DMA((2, blocks)),
+            pltpu.SemaphoreType.DMA((2, blocks)),
+        ],
+        compiler_params=pltpu.CompilerParams(vmem_limit_bytes=56 * 1024 * 1024),
     )(owners, small_sum, energy, new_weight, new_moment, *adam)
 
 

time: 272 us -> 83.5 us (0.31)
  Pallas kernels: 271 us -> 82.7 us
    pallas_call x1, Pallas kernels: 194 us -> 8.05 us  [linked_device(): pl.pallas_call(finish_kernel, out_shape=(jax.ShapeDtypeStruct(block_shape...]
where the time goes in v4:
time: 83.5 us; the launch traced here: 83.3 us
  Pallas kernels  82.7 us (99%)
    pallas_call x1, Pallas kernels, linked_device(): pl.pallas_call(linked_kernel, out_shape=(jax.ShapeDtypeStruct(block_shape...  74.6 us
    pallas_call x1, Pallas kernels, linked_device(): pl.pallas_call(finish_kernel, out_shape=(jax.ShapeDtypeStruct(block_shape...  8.05 us

profile of v4, /device:TPU:0, one launch (start us, length us, event | category | flops | bytes accessed | tf_op | source)
XLA Modules:
  0.0 83.3 jit_solution(17423346136400774004)
XLA Ops:
  0.6 74.6 %shard_map.247 = (bf16[6,64,4096]{2,1,0:T(8,128)(2,1)}, bf16[6,64,4096]{2,1,0:T(8,128)(2,1)}, bf16[48,4096]{1,0:T(8,128)(2,1)}, f32[8,128]{1,0:T(8,128)}) custom-call(bf16[2,2048]{1,0:T(2,128)(2,1)} %bitcast.6, bf16[2,128]{1,0:T(2,128)(2,1)} %bitcast.7, bf16[6,64,4096]{2,1,0:T(8,128)(2,1)} %bitcast.4, bf16[32,4096]{1,0:T(8,128)(2,1)} %bitcast.5, ...), custom_call_target="tpu_custom_call" | custom-call | tf_op jit(solution)/shard_map/pallas_call | solution.py:579
  75.3 8.0 %shard_map.248 = (bf16[6,64,4096]{2,1,0:T(8,128)(2,1)}, bf16[6,64,4096]{2,1,0:T(8,128)(2,1)}, f32[1,3]{1,0:T(1,128)}, bf16[32,4096]{1,0:T(8,128)(2,1)}, f32[32,4...) custom-call(s32[6]{0:T(128)} %owners.1, ...), custom_call_target="tpu_custom_call" | custom-call | tf_op jit(solution)/shard_map/pallas_call | solution.py:622
